TPU v7x, 32 devices: a whole 2x2x4 slice. The times are simulated.
32 devices in a mesh: rep: 2 (over x), node: 2 (over core), local: 8 (over z, y).
Axes of the slice: x: 2, y: 2, z: 4, core: 2. Of those that a mesh axis runs over, the one named last changes fastest.
Arguments:
- tokens: bfloat16 [4096, 3584], P(('rep', 'node', 'local')), parts along dimension 0, may hold values from -6 to 6
- grads: bfloat16 [4096, 8, 1024], P(('rep', 'node', 'local')), parts along dimension 0, may hold values from -6 to 6
- route_weights: float32 [4096, 8], P(('rep', 'node', 'local')), parts along dimension 0, may hold values from 0.1 to 1
- route_ids: int32 [4096, 8], P(('rep', 'node', 'local')), parts along dimension 0, may hold values from 0 to 1, as said below
- group_picks: int32 [4096, 4], P(('rep', 'node', 'local')), parts along dimension 0, may hold values from 0 to 7, as said below
- frozen_up: bfloat16 [16, 3584, 1024], P(('node', 'local')), may hold values from -0.09375 to 0.09375
- factor_a: bfloat16 [16, 3584, 32], P(('node', 'local')), may hold values from -0.09375 to 0.09375
- factor_b: bfloat16 [16, 32, 1024], P(('node', 'local')), may hold values from -1 to 1
Outputs:
- input_grad: bfloat16 [4096, 3584], P(('rep', 'node', 'local')), parts along dimension 0
- grad_a: float32 [32, 3584, 32], P(('rep', 'node', 'local')), parts along dimension 0
- grad_b: float32 [32, 32, 1024], P(('rep', 'node', 'local')), parts along dimension 0
There are 2 independent parts, one for each index of `rep`. A program takes and returns all parts, laid end to end along the dimension named above; an argument that names none is the same for every part. Nothing has to cross between parts.
Inputs may be any that keep to these rules, and one draw needn't show every extreme that they name: `route_ids`: A token's 4 groups are distinct, so its 8 experts are distinct. Among the tokens of one device no expert is named by more than 80 routes; in every draw one group is picked by exactly 80 tokens of every device, and each of its 2 experts is named by exactly 80 routes of every device. The experts of one group named by one device's routes differ in their counts by at most one. `group_picks`: no group is picked by more than 80 tokens of one device.
All inputs are finite; a program needn't handle non-finite values.
Results may differ from a plain program's by a relative error of at most 0.0058.
Values may be sent and summed in bfloat16 or wider, within the bound.
A program may use at most 192 MiB of HBM per device.

v0:
```python
import jax
import jax.numpy as jnp
from jax import lax
from jax.sharding import PartitionSpec as P

GROUPS = 8


adapter_scale_factor = 0.25
weight_gradient_total = 1.0 / 32.0


def slot_ranks(expert_flat, device_count):
    onehot = (expert_flat[:, None] == jnp.arange(device_count, dtype=jnp.int32)[None, :]).astype(
        jnp.int32
    )
    earlier = jnp.cumsum(onehot, axis=0) - onehot
    return jnp.sum(earlier * onehot, axis=1)


def slot_grads(arrived, arrived_grads, frozen, first, second):
    lead = arrived.shape[:-1]
    input_rows = arrived.reshape(-1, arrived.shape[-1])
    gradient_rows = arrived_grads.reshape(-1, arrived_grads.shape[-1])
    rank_space_rows = lax.dot_general(
        gradient_rows, second, (((1,), (1,)), ((), ())), preferred_element_type=jnp.float32
    ).astype(jnp.bfloat16)
    joined_rows = jnp.concatenate([gradient_rows, rank_space_rows], axis=1)
    joined_weight = jnp.concatenate([frozen, first * adapter_scale_factor], axis=1)
    route_gradient = lax.dot_general(
        joined_rows, joined_weight, (((1,), (1,)), ((), ())), preferred_element_type=jnp.float32
    ).astype(jnp.bfloat16)
    projected_rows = jnp.dot(input_rows, first, preferred_element_type=jnp.float32).astype(
        jnp.bfloat16
    )
    return (
        route_gradient.reshape(lead + (frozen.shape[0],)),
        rank_space_rows.reshape(lead + (second.shape[0],)),
        projected_rows.reshape(lead + (second.shape[0],)),
    )


def send_buffers(tokens, scaled, target, device_count, slot_most):
    tok_rows, width = tokens.shape
    pair_count, hidden = scaled.shape
    topk = pair_count // tok_rows
    scaled_pad = jnp.concatenate([scaled, jnp.zeros((1, hidden), jnp.bfloat16)], axis=0)
    tokens_pad = jnp.concatenate([tokens, jnp.zeros((1, width), jnp.bfloat16)], axis=0)
    source = jnp.full((device_count * slot_most,), pair_count, jnp.int32)
    source = source.at[target].set(jnp.arange(pair_count, dtype=jnp.int32))
    owner = jnp.where(source < pair_count, source // topk, tok_rows)
    send_x = tokens_pad[owner].reshape(device_count, slot_most, width)
    send_g = scaled_pad[source].reshape(device_count, slot_most, hidden)
    return (send_x, send_g)


def body(tokens, grads, route_weights, route_ids, group_picks, frozen_up, factor_a, factor_b):
    tok_rows = tokens.shape[0]
    topk = route_ids.shape[1]
    width = tokens.shape[1]
    hidden = grads.shape[2]
    node_count = lax.axis_size("node")
    local_count = lax.axis_size("local")
    device_count = node_count * local_count
    group_size = device_count // GROUPS
    slot_most = 2 * (5 * tok_rows // 8) // group_size
    pair_count = tok_rows * topk
    frozen = frozen_up[0]
    first = factor_a[0]
    second = factor_b[0]
    experts = jnp.repeat(group_picks, 2, axis=1) * group_size + route_ids
    expert_flat = experts.reshape(-1)
    ranks = slot_ranks(expert_flat, device_count)
    target = expert_flat * slot_most + ranks
    scaled = (
        (grads.astype(jnp.float32) * route_weights[:, :, None])
        .astype(jnp.bfloat16)
        .reshape(pair_count, hidden)
    )
    send_x, send_g = send_buffers(tokens, scaled, target, device_count, slot_most)
    pieces = (
        lax.all_to_all(send_x, ("node", "local"), split_axis=0, concat_axis=0, tiled=True),
        lax.all_to_all(send_g, ("node", "local"), split_axis=0, concat_axis=0, tiled=True),
    )
    route_gradient, rank_space_rows, projected_rows = slot_grads(
        pieces[0], pieces[1], frozen, first, second
    )
    arrived, arrived_grads, route_gradient, rank_space_rows, projected_rows = (
        pieces[0],
        pieces[1],
        route_gradient,
        rank_space_rows,
        projected_rows,
    )
    input_rows = arrived.reshape(-1, width)
    gradient_rows = arrived_grads.reshape(-1, hidden)
    first_factor_gradient = (
        weight_gradient_total
        * adapter_scale_factor
        * lax.dot_general(
            input_rows,
            rank_space_rows.reshape(-1, rank_space_rows.shape[-1]),
            (((0,), (0,)), ((), ())),
            preferred_element_type=jnp.float32,
        )
    )
    second_factor_gradient = (
        weight_gradient_total
        * adapter_scale_factor
        * lax.dot_general(
            projected_rows.reshape(-1, projected_rows.shape[-1]),
            gradient_rows,
            (((0,), (0,)), ((), ())),
            preferred_element_type=jnp.float32,
        )
    )
    returned = lax.all_to_all(
        route_gradient, ("node", "local"), split_axis=0, concat_axis=0, tiled=True
    )
    picked = returned.reshape(-1, width)[target]
    input_grad = jnp.sum(picked.reshape(tok_rows, topk, width).astype(jnp.float32), axis=1).astype(
        jnp.bfloat16
    )
    return (input_grad, first_factor_gradient[None], second_factor_gradient[None])


def solution(mesh):
    return jax.shard_map(
        body,
        mesh=mesh,
        in_specs=(
            P(("rep", "node", "local"), None),
            P(("rep", "node", "local"), None, None),
            P(("rep", "node", "local"), None),
            P(("rep", "node", "local"), None),
            P(("rep", "node", "local"), None),
            P(("node", "local"), None, None),
            P(("node", "local"), None, None),
            P(("node", "local"), None, None),
        ),
        out_specs=(
            P(("rep", "node", "local"), None),
            P(("rep", "node", "local"), None, None),
            P(("rep", "node", "local"), None, None),
        ),
        check_vma=False,
    )
```

profile of v0, /device:TPU:8, one launch (start us, length us, event | category | flops | bytes accessed | tf_op | source)
XLA Modules:
  0.0 522.7 jit_solution(481885304762950734)
XLA Ops:
  0.6 0.0 copy-start
  0.6 0.7 broadcast_multiply_fusion.1
  1.4 0.7 broadcast_multiply_fusion
  2.1 0.1 copy.18
  2.2 0.1 eq.29
  2.3 0.1 eq.25
  2.4 4.5 reduce-window.6
  6.9 0.1 slice.14
  7.0 0.1 copy.20
  7.1 0.1 copy.21
  7.2 0.1 broadcast_add_fusion
  7.3 0.1 copy.17
  7.4 0.1 mul.62
  7.6 4.3 scatter_custom_fusion
  11.9 0.8 copy.16
  12.7 2.0 fusion.7
  14.7 0.2 concatenate.12
  14.9 0.0 copy-start.2
  14.9 5.1 gather_fusion
  20.0 6.3 %all-to-all-start = ((bf16[16,80,1024]{2,1,0:T(8,128)(2,1)}), bf16[16,80,1024]{2,1,0:T(8,128)(2,1)}, u32[]{:S(2)}, u32[]{:S(2)}) async-start(bf16[16,80,1024]{2,1,0:T(8,128)(2,1)} %bitcast.50), calls=%async_computation | async-start | bytes 5242880 | tf_op jit(solution)/shard_map/all_to_all | solution.py:83
  26.3 0.0 copy-done.2
  26.3 0.1 concatenate.15
  26.4 7.9 %gather_fusion.2 = bf16[1280,3584]{1,0:T(8,128)(2,1)} fusion(bf16[129,3584]{1,0:T(8,128)(2,1)S(1)} %concatenate.15, s32[2048]{0:T(1024)S(1)} %get-tuple-element.7), kind=kCustom, calls=%fused_computation.2 | custom fusion | bytes 18355200 | tf_op jit(solution)/shard_map/gather | solution.py:52
  34.3 51.9 %all-to-all-done = bf16[16,80,1024]{2,1,0:T(8,128)(2,1)} async-done(((bf16[16,80,1024]{2,1,0:T(8,128)(2,1)}), bf16[16,80,1024]{2,1,0:T(8,128)(2,1)}, u32[]{:S(2)}, u32[]{:S(2)}) %all-to-all-start) | async-done | bytes 2621472 | tf_op jit(solution)/shard_map/all_to_all | solution.py:83
  86.2 0.0 copy-start.3
  86.2 4.8 all-to-all-start.2
  91.1 0.0 copy-done.3
  91.1 0.4 copy.23
  91.5 0.0 copy-done
  91.6 2.6 convolution_convert_fusion.2
  94.2 0.2 copy.22
  94.4 17.4 %convolution_convert_fusion = bf16[1280,3584]{1,0:T(8,128)(2,1)} fusion(bf16[3584,32]{1,0:T(8,128)(2,1)S(1)} %copy.23, bf16[3584,1024]{1,0:T(8,128)(2,1)} %bitcast.58, bf16[1280,32]{1,0:T(8,128)(2,1)S(1)} %copy.22, bf16[1280,1024]{1,0:T(8,128)(2,1)} %bitcast.7), kind=kOutput, calls=%fused_computation.4 | convolution fusion | flops 9713975296 | bytes 19447808 | tf_op jit(solution)/shard_map/dot_general | solution.py:30
  111.8 179.0 %all-to-all-done.2 = bf16[16,80,3584]{2,1,0:T(8,128)(2,1)} async-done(((bf16[16,80,3584]{2,1,0:T(8,128)(2,1)}), bf16[16,80,3584]{2,1,0:T(8,128)(2,1)}, u32[]{:S(2)}, u32[]{:S(2)}) %all-to-all-start.2) | async-done | bytes 9175072 | tf_op jit(solution)/shard_map/all_to_all | solution.py:82
  290.8 4.9 all-to-all-start.1
  295.6 6.0 %fusion.3 = f32[1,3584,32]{1,2,0:T(8,128)} fusion(bf16[1280,32]{0,1:T(8,128)(2,1)S(1)} %convolution_convert_fusion.2, bf16[1280,3584]{1,0:T(8,128)(2,1)} %bitcast.15), kind=kOutput, calls=%fused_computation.10 | convolution fusion | flops 293715968 | bytes 9715712 | tf_op jit(solution)/shard_map/dot_general | solution.py:100
  301.7 8.4 %fusion.10 = f32[1,32,1024]{2,1,0:T(8,128)} fusion(bf16[1280,1024]{1,0:T(8,128)(2,1)} %bitcast.7, bf16[1280,3584]{1,0:T(8,128)(2,1)} %bitcast.15, bf16[1,3584,32]{1,2,0:T(8,128)(2,1)S(1)} %copy-done.3), kind=kOutput, calls=%fused_computation.20 | convolution fusion | flops 377561088 | bytes 12156928 | tf_op jit(solution)/shard_map/dot_general | solution.py:110
  310.1 185.0 %all-to-all-done.1 = bf16[16,80,3584]{2,1,0:T(8,128)(2,1)} async-done(((bf16[16,80,3584]{2,1,0:T(8,128)(2,1)}), bf16[16,80,3584]{2,1,0:T(8,128)(2,1)}, u32[]{:S(2)}, u32[]{:S(2)}) %all-to-all-start.1) | async-done | bytes 9175072 | tf_op jit(solution)/shard_map/all_to_all | solution.py:117
  495.2 0.0 copy-start.1
  495.2 18.6 %gather_fusion.1 = bf16[1024,3584]{1,0:T(8,128)(2,1)} fusion(bf16[1280,3584]{1,0:T(8,128)(2,1)} %bitcast.12, s32[1024]{0:T(1024)S(1)} %broadcast_clamp_fusion), kind=kCustom, calls=%fused_computation.1 | custom fusion | bytes 14684160 | tf_op jit(solution)/shard_map/gather | solution.py:120
  513.8 8.9 %bitcast_reduce_fusion = bf16[128,3584]{1,0:T(8,128)(2,1)} fusion(bf16[1024,3584]{1,0:T(8,128)(2,1)} %gather_fusion.1), kind=kLoop, calls=%fused_computation.8 | loop fusion | flops 3211264 | bytes 8257536 | tf_op jit(solution)/shard_map/reduce_sum | solution.py:121
  522.7 0.0 copy-done.1
  (11 shorter events, 0.1 us)
Async XLA Ops:
  0.6 90.9 %copy-start = (bf16[1,32,1024]{2,1,0:T(8,128)(2,1)S(1)}, bf16[1,32,1024]{2,1,0:T(8,128)(2,1)}, u32[]{:S(2)}) copy-start(bf16[1,32,1024]{2,1,0:T(8,128)(2,1)} %param.15) | copy-start | bytes 196612
  14.9 11.4 %copy-start.2 = (bf16[128,3584]{1,0:T(8,128)(2,1)S(1)}, bf16[128,3584]{1,0:T(8,128)(2,1)}, u32[]{:S(2)}) copy-start(bf16[128,3584]{1,0:T(8,128)(2,1)} %param.8) | copy-start | bytes 2752516
  20.0 66.2 %all-to-all-start = ((bf16[16,80,1024]{2,1,0:T(8,128)(2,1)}), bf16[16,80,1024]{2,1,0:T(8,128)(2,1)}, u32[]{:S(2)}, u32[]{:S(2)}) async-start(bf16[16,80,1024]{2,1,0:T(8,128)(2,1)} %bitcast.50), calls=%async_computation | async-start | bytes 5242880 | tf_op jit(solution)/shard_map/all_to_all | solution.py:83
  86.2 4.8 copy-start.3
  86.2 204.5 %all-to-all-start.2 = ((bf16[16,80,3584]{2,1,0:T(8,128)(2,1)}), bf16[16,80,3584]{2,1,0:T(8,128)(2,1)}, u32[]{:S(2)}, u32[]{:S(2)}) async-start(bf16[16,80,3584]{2,1,0:T(8,128)(2,1)} %bitcast.49), calls=%async_computation.2 | async-start | bytes 18350080 | tf_op jit(solution)/shard_map/all_to_all | solution.py:82
  290.8 204.4 %all-to-all-start.1 = ((bf16[16,80,3584]{2,1,0:T(8,128)(2,1)}), bf16[16,80,3584]{2,1,0:T(8,128)(2,1)}, u32[]{:S(2)}, u32[]{:S(2)}) async-start(bf16[16,80,3584]{2,1,0:T(8,128)(2,1)} %bitcast.51), calls=%async_computation.1 | async-start | bytes 18350080 | tf_op jit(solution)/shard_map/all_to_all | solution.py:117
  495.2 27.5 %copy-start.1 = (bf16[1,32,1024]{2,1,0:T(8,128)(2,1)S(1)}, bf16[1,32,1024]{2,1,0:T(8,128)(2,1)}, u32[]{:S(2)}) copy-start(bf16[1,32,1024]{2,1,0:T(8,128)(2,1)} %param.15) | copy-start | bytes 196612
where the time goes:
time: 523 us
  waiting for transfers between devices  416 us (80%)
  local copies, waits for them, and re-layouts  38.5 us (7%)
  matrix products  34.4 us (7%)
  other arithmetic  17.1 us (3%)
  starting transfers between devices  16 us (3%)
    all_to_all x1, waiting for transfers between devices, body(): lax.all_to_all(route_gradient, ('node', 'local'), split_axis=0, concat_ax...  185 us
    all_to_all x1, waiting for transfers between devices, body(): lax.all_to_all(send_x, ('node', 'local'), split_axis=0, concat_axis=0, ti...  179 us
    all_to_all x1, waiting for transfers between devices, body(): lax.all_to_all(send_g, ('node', 'local'), split_axis=0, concat_axis=0, ti...  51.9 us
    gather x1, local copies, waits for them, and re-layouts, body(): picked = returned.reshape(-1, width)[target]  18.6 us
    dot_general x1, matrix products, slot_grads(): lax.dot_general(joined_rows, joined_weight, (((1,), (1,)), ((), ())), pre...  17.4 us
  transfers between devices with their start and end apart: 3, of which 3 were waited for; matrix products, arithmetic and copies ran while one was open for 8% of the time, Pallas kernels for 0%

commit v1 on v0

--- a/solution.py
+++ b/solution.py
@@ -54,7 +54,7 @@
     return (send_x, send_g)
 
 
-def body(tokens, grads, route_weights, route_ids, group_picks, frozen_up, factor_a, factor_b):
+def sparse_body(tokens, grads, route_weights, route_ids, group_picks, frozen_up, factor_a, factor_b):
     tok_rows = tokens.shape[0]
     topk = route_ids.shape[1]
     width = tokens.shape[1]
@@ -124,6 +124,98 @@
     return (input_grad, first_factor_gradient[None], second_factor_gradient[None])
 
 
+def scale_routes(grads, route_weights):
+    pair_count = grads.shape[0] * grads.shape[1]
+    return (
+        (grads.astype(jnp.float32) * route_weights[:, :, None])
+        .astype(jnp.bfloat16)
+        .reshape(pair_count, grads.shape[2])
+    )
+
+
+def dense_body(tokens, grads, route_weights, route_ids, group_picks, frozen_up, factor_a, factor_b):
+    tok_rows, width = tokens.shape
+    topk = route_ids.shape[1]
+    hidden = grads.shape[2]
+    rank = factor_b.shape[1]
+    axes = ("node", "local")
+    device_count = lax.axis_size("node") * lax.axis_size("local")
+    me = lax.axis_index("node") * lax.axis_size("local") + lax.axis_index("local")
+    group_size = device_count // GROUPS
+    slot_most = 2 * (5 * tok_rows // 8) // group_size
+    f32, bf16 = jnp.float32, jnp.bfloat16
+    experts = jnp.repeat(group_picks, 2, axis=1) * group_size + route_ids
+    expert_flat = experts.reshape(-1)
+    first_t = factor_a[0].T
+    second = factor_b[0]
+    table = jnp.zeros((rank, tok_rows), bf16).at[:topk].set(experts.T.astype(bf16))
+    shared = lax.all_gather(
+        jnp.concatenate([first_t, second, table], axis=1), axes, axis=0, tiled=True
+    )
+    all_first = shared[:, :width]
+    all_second = shared[:, width : width + hidden]
+    tables = shared[:, width + hidden :].reshape(device_count, rank, tok_rows)[:, :topk]
+
+    ids = jnp.arange(device_count, dtype=jnp.int32)
+    member = (experts[:, :, None] == ids[None, None, :]).any(axis=1)
+    order = jnp.cumsum(member.astype(jnp.int32), axis=0) - 1
+    ranks = jnp.sum(jnp.where(experts[:, :, None] == ids, order[:, None, :], 0), axis=2)
+    target = experts * slot_most + ranks
+    scaled = scale_routes(grads, route_weights)
+    slots = jnp.arange(device_count * slot_most, dtype=jnp.int32)
+    pack = (target.reshape(1, -1) == slots[:, None]).astype(bf16)
+    send_g = jnp.dot(pack, scaled, preferred_element_type=f32).astype(bf16)
+    arrived = lax.all_to_all(
+        send_g.reshape(device_count, slot_most, hidden), axes, split_axis=0, concat_axis=0, tiled=True
+    )
+
+    owner_mask = expert_flat[:, None] == jnp.repeat(ids, rank)[None, :]
+    middle = lax.dot_general(scaled, all_second, (((1,), (1,)), ((), ())), preferred_element_type=f32)
+    middle = jnp.where(owner_mask, middle, 0.0).reshape(tok_rows, topk, -1).sum(axis=1).astype(bf16)
+    projected = lax.dot_general(
+        tokens, all_first, (((1,), (1,)), ((), ())), preferred_element_type=f32
+    ).astype(bf16)
+    projected = jnp.where(
+        owner_mask.reshape(tok_rows, topk, -1), projected[:, None, :], jnp.zeros((), bf16)
+    ).reshape(tok_rows * topk, -1)
+    share_a = lax.dot_general(middle, tokens, (((0,), (0,)), ((), ())), preferred_element_type=f32)
+    share_b = lax.dot_general(projected, scaled, (((0,), (0,)), ((), ())), preferred_element_type=f32)
+    shares = jnp.concatenate([share_a.astype(bf16), share_b.astype(bf16)], axis=1)
+    factor_gradients = lax.psum_scatter(shares, "node", scatter_dimension=0, tiled=True)
+    factor_gradients = lax.psum_scatter(factor_gradients, "local", scatter_dimension=0, tiled=True)
+    factor_gradients = factor_gradients.astype(f32) * (weight_gradient_total * adapter_scale_factor)
+
+    mine = (tables == me.astype(bf16)).any(axis=1)
+    place = jnp.cumsum(mine.astype(jnp.int32), axis=1) - 1
+    unpack = (
+        mine[:, :, None] & (place[:, :, None] == jnp.arange(slot_most, dtype=jnp.int32))
+    ).astype(bf16)
+    rows = (
+        lax.dot_general(unpack, arrived, (((2,), (1,)), ((0,), (0,))), preferred_element_type=f32)
+        .astype(bf16)
+        .reshape(device_count * tok_rows, hidden)
+    )
+    row_middle = lax.dot_general(
+        rows, second, (((1,), (1,)), ((), ())), preferred_element_type=f32
+    ).astype(bf16)
+    joined_rows = jnp.concatenate([rows, row_middle], axis=1)
+    joined_weight = jnp.concatenate([frozen_up[0], factor_a[0] * adapter_scale_factor], axis=1)
+    partial = lax.dot_general(
+        joined_rows, joined_weight, (((1,), (1,)), ((), ())), preferred_element_type=f32
+    ).astype(bf16)
+    partial = lax.psum_scatter(partial, "node", scatter_dimension=0, tiled=True)
+    input_grad = lax.psum_scatter(partial, "local", scatter_dimension=0, tiled=True)
+    return (input_grad, factor_gradients[:, :width].T[None], factor_gradients[:, width:][None])
+
+
+def body(tokens, grads, route_weights, route_ids, group_picks, frozen_up, factor_a, factor_b):
+    tok_rows = tokens.shape[0]
+    group_size = lax.axis_size("node") * lax.axis_size("local") // GROUPS
+    slot_most = 2 * (5 * tok_rows // 8) // group_size
+    plan = dense_body if tok_rows <= 2 * slot_most else sparse_body
+    return plan(tokens, grads, route_weights, route_ids, group_picks, frozen_up, factor_a, factor_b)
+
+
 def solution(mesh):
     return jax.shard_map(
         body,

time: 523 us -> 420 us (0.80)
  waiting for transfers between devices: 416 us -> 336 us
  local copies, waits for them, and re-layouts: 38.5 us -> 8.83 us
  between operations: 0.81 us -> 13.9 us
  starting transfers between devices: 16 us -> 4.45 us
  matrix products: 34.4 us -> 43 us
  other arithmetic: 17.1 us -> 10.9 us
    all_to_all x3 -> x1, waiting for transfers between devices: 416 us -> 53.9 us  [dense_body(): lax.all_to_all(send_g.reshape(device_count, slot_most, hidden), axes, spl...]
    reduce_scatter x0 -> x4, waiting for transfers between devices: none -> 229 us  [the longest x1 133 us: dense_body(): lax.psum_scatter(partial, 'local', scatter_dimension=0, tiled=True)]
    all_gather x0 -> x1, waiting for transfers between devices: none -> 52.2 us  [dense_body(): lax.all_gather(jnp.concatenate([first_t, second, table], axis=1), axes, a...]
    gather x3 -> x0, local copies, waits for them, and re-layouts: 31.6 us -> none  [the longest x1 18.6 us: body(): picked = returned.reshape(-1, width)[target]]
    all_to_all x3 -> x1, starting transfers between devices: 16 us -> 4.07 us  [dense_body(): lax.all_to_all(send_g.reshape(device_count, slot_most, hidden), axes, spl...]
    reduce_sum x2 -> x1, other arithmetic: 8.96 us -> 0.02 us  [dense_body(): jnp.sum(jnp.where(experts[:, :, None] == ids, order[:, None, :], 0), axis=2)]
    dot_general x4 -> x8, matrix products: 34.4 us -> 43 us  [the longest x1 25.5 us: dense_body(): lax.dot_general(joined_rows, joined_weight, (((1,), (1,)), ((), ())), pre...]
  transfers between devices with their start and end apart: 3 -> 6, of which waited for: 3 -> 5; matrix products, arithmetic and copies ran while one was open for 8% -> 11% of each run, Pallas kernels for 0% -> 0%
where the time goes in v1:
time: 420 us; the launch traced here: 417 us
  waiting for transfers between devices  336 us (80%)
  matrix products  43 us (10%)
  between operations  13.9 us (3%)
  other arithmetic  10.9 us (3%)
  local copies, waits for them, and re-layouts  8.83 us (2%)
  starting transfers between devices  4.45 us (1%)
    reduce_scatter x1, waiting for transfers between devices, dense_body(): lax.psum_scatter(partial, 'local', scatter_dimension=0, tiled=True)  133 us
    reduce_scatter x1, waiting for transfers between devices, dense_body(): lax.psum_scatter(factor_gradients, 'local', scatter_dimension=0, tiled=True)  73.3 us
    all_to_all x1, waiting for transfers between devices, dense_body(): lax.all_to_all(send_g.reshape(device_count, slot_most, hidden), axes, spl...  53.9 us
    all_gather x1, waiting for transfers between devices, dense_body(): lax.all_gather(jnp.concatenate([first_t, second, table], axis=1), axes, a...  52.2 us
    dot_general x1, matrix products, dense_body(): lax.dot_general(joined_rows, joined_weight, (((1,), (1,)), ((), ())), pre...  25.5 us
    reduce_scatter x1, waiting for transfers between devices, dense_body(): partial = lax.psum_scatter(partial, 'node', scatter_dimension=0, tiled=True)  22.6 us
  transfers between devices with their start and end apart: 6, of which 5 were waited for; matrix products, arithmetic and copies ran while one was open for 11% of the time, Pallas kernels for 0%

profile of v1, /device:TPU:8, one launch (start us, length us, event | category | flops | bytes accessed | tf_op | source)
XLA Modules:
  0.0 417.0 jit_solution(6114947736259028418)
XLA Ops:
  7.2 0.0 all-gather.2.cloned.1.call-start
  7.2 0.8 broadcast_multiply_fusion
  8.0 0.7 convert_bitcast_fusion
  8.7 1.7 fusion.36
  10.4 0.0 all-gather.2.cloned.1.call-update
  10.4 0.0 reduce-scatter.9.cloned.1.call-start
  10.5 0.1 copy.27
  10.6 0.1 eq.94
  10.7 0.1 copy.21
  10.8 0.2 reduce_window_sum.23
  11.0 0.1 copy.22
  11.0 0.1 eq.92
  11.1 0.8 copy.24
  11.9 2.0 multiply_convert_fusion
  13.9 52.2 %all-gather.2.cloned.1.call-done = bf16[512,4736]{1,0:T(8,128)(2,1)} async-done(((bf16[32,4736]{1,0:T(8,128)(2,1)}), bf16[512,4736]{1,0:T(8,128)(2,1)}) %all-gather.2.cloned.1.call-update) | async-done | bytes 4849680 | tf_op jit(solution)/shard_map/all_gather | solution.py:152
  66.1 3.1 fusion.23
  69.3 2.8 bitcast_convert_fusion
  72.1 2.9 bitcast_reduce_fusion
  75.0 1.1 convolution_convert_fusion.1
  76.1 2.5 pad_maximum_fusion
  78.7 0.1 copy.23
  78.8 0.1 eq.88
  78.9 4.2 fusion.7
  83.0 4.1 all-to-all-start
  87.1 0.2 reduce-scatter.5.cloned.1.call-start
  87.3 1.7 bitcast_multiply_fusion
  89.0 2.2 copy.26
  91.2 0.9 slice.40
  92.2 0.6 copy-done.4
  92.8 0.3 reduce_window_sum.22
  93.1 53.9 %all-to-all-done = bf16[16,80,1024]{2,1,0:T(8,128)(2,1)S(1)} async-done(((bf16[16,80,1024]{2,1,0:T(8,128)(2,1)}), bf16[16,80,1024]{2,1,0:T(8,128)(2,1)S(1)}, u32[]{:S(2)}, u32[]{:S(2)}) %all-to-all-start) | async-done | bytes 2621472 | tf_op jit(solution)/shard_map/all_to_all | solution.py:168
  147.0 2.0 convolution_convert_fusion.2
  149.0 2.0 copy-done.1
  150.9 1.3 convolution_convert_fusion.3
  152.3 0.3 copy.25
  152.6 25.5 %convolution_convert_fusion = bf16[2048,3584]{1,0:T(8,128)(2,1)} fusion(bf16[3584,32]{1,0:T(8,128)(2,1)S(1)} %copy-done.2, bf16[3584,1024]{1,0:T(8,128)(2,1)} %bitcast.45, bf16[2048,32]{1,0:T(8,128)(2,1)S(1)} %copy.25, bf16[2048,1024]{1,0:T(8,128)(2,1)} %bitcast.39), kind=kOutput, calls=%fused_computation | convolution fusion | flops 15533277184 | bytes 26574848 | tf_op jit(solution)/shard_map/dot_general | solution.py:203
  178.1 0.0 reduce-scatter.5.cloned.1.call-update
  178.1 0.0 reduce-scatter.11.cloned.1.call-start
  178.2 0.0 reduce-scatter.9.cloned.1.call-done
  178.2 0.5 reduce-scatter.11.cloned.1.call-update
  178.7 0.0 reduce-scatter.7.cloned.1.call-start
  178.7 22.6 %reduce-scatter.5.cloned.1.call-done = bf16[1024,3584]{1,0:T(8,128)(2,1)} async-done(((bf16[2048,3584]{1,0:T(8,128)(2,1)}), bf16[1024,3584]{1,0:T(8,128)(2,1)}) %reduce-scatter.5.cloned.1.call-update) | async-done | bytes 7340048 | tf_op jit(solution)/shard_map/reduce_scatter | solution.py:206
  201.4 0.0 reduce-scatter.7.cloned.1.call-update
  201.4 73.3 %reduce-scatter.11.cloned.1.call-done = bf16[32,4608]{1,0:T(8,128)(2,1)} async-done(((bf16[256,4608]{1,0:T(8,128)(2,1)}), bf16[32,4608]{1,0:T(8,128)(2,1)}) %reduce-scatter.11.cloned.1.call-update) | async-done | bytes 294928 | tf_op jit(solution)/shard_map/reduce_scatter | solution.py:185
  274.7 1.0 convert_multiply_fusion
  275.7 0.7 slice_bitcast_fusion.1
  276.4 0.8 slice_bitcast_fusion
  277.1 133.3 %reduce-scatter.7.cloned.1.call-done = bf16[128,3584]{1,0:T(8,128)(2,1)} async-done(((bf16[1024,3584]{1,0:T(8,128)(2,1)}), bf16[128,3584]{1,0:T(8,128)(2,1)}) %reduce-scatter.7.cloned.1.call-update) | async-done | bytes 917520 | tf_op jit(solution)/shard_map/reduce_scatter | solution.py:207
  (19 shorter events, 0.1 us)
Async XLA Ops:
  7.2 59.0 %copy-start = (bf16[128,3584]{1,0:T(8,128)(2,1)S(1)}, bf16[128,3584]{1,0:T(8,128)(2,1)}, u32[]{:S(2)}) copy-start(bf16[128,3584]{1,0:T(8,128)(2,1)} %param.10) | copy-start | bytes 2752516
  7.2 58.9 %all-gather.2.cloned.1.call-start = ((), (), s32[]{:S(2)}) async-start(), calls=%async_computation.5 | async-start | bytes 5152768 | tf_op jit(solution)/shard_map/all_gather | solution.py:152
  10.4 167.8 %reduce-scatter.9.cloned.1.call-start = ((), (), s32[]{:S(2)}) async-start(), calls=%async_computation.8 | async-start | bytes 7077888 | tf_op jit(solution)/shard_map/reduce_scatter | solution.py:184
  83.0 63.9 %all-to-all-start = ((bf16[16,80,1024]{2,1,0:T(8,128)(2,1)}), bf16[16,80,1024]{2,1,0:T(8,128)(2,1)S(1)}, u32[]{:S(2)}, u32[]{:S(2)}) async-start(bf16[16,80,1024]{2,1,0:T(8,128)(2,1)} %bitcast.40), calls=%async_computation | async-start | bytes 5242880 | tf_op jit(solution)/shard_map/all_to_all | solution.py:168
  87.1 114.3 %reduce-scatter.5.cloned.1.call-start = ((), (), s32[]{:S(2)}) async-start(), calls=%async_computation.6 | async-start | bytes 22020096 | tf_op jit(solution)/shard_map/reduce_scatter | solution.py:206
  92.2 0.6 copy-start.4
  147.0 4.0 copy-start.3
  149.0 2.0 copy-start.1
  149.0 3.6 copy-start.2
  178.1 96.6 %reduce-scatter.11.cloned.1.call-start = ((), (), s32[]{:S(2)}) async-start(), calls=%async_computation.9 | async-start | bytes 2654208 | tf_op jit(solution)/shard_map/reduce_scatter | solution.py:185
  178.7 231.7 %reduce-scatter.7.cloned.1.call-start = ((), (), s32[]{:S(2)}) async-start(), calls=%async_computation.7 | async-start | bytes 8257536 | tf_op jit(solution)/shard_map/reduce_scatter | solution.py:207
Sparse Core Ops, SparseCore 0:
  10.8 55.2 all-gather.1
  78.8 11.3 reduce-scatter.8
  178.2 23.1 reduce-scatter.4
  205.1 69.4 reduce-scatter.10
  279.1 131.2 reduce-scatter.6

commit v2 on v1

--- a/solution.py
+++ b/solution.py
@@ -1,6 +1,9 @@
+import functools
 import jax
 import jax.numpy as jnp
 from jax import lax
+from jax.experimental import pallas as pl
+from jax.experimental.pallas import tpu as pltpu
 from jax.sharding import PartitionSpec as P
 
 GROUPS = 8
@@ -124,6 +127,261 @@
     return (input_grad, first_factor_gradient[None], second_factor_gradient[None])
 
 
+MESH = pl.DeviceIdType.MESH
+
+
+def tile_of(width):
+    for tile in (512, 256, 128):
+        if width % tile == 0:
+            return tile
+    return width
+
+
+def visit_order(count):
+    table = []
+    for z in range(count):
+        above, below = list(range(count - 1, z, -1)), list(range(z))
+        order = []
+        while above or below:
+            first, other = (above, below) if len(above) >= len(below) else (below, above)
+            order.append(first.pop(0))
+            if other:
+                order.append(other.pop(0))
+        table.append(order + [z])
+    return table
+
+
+def return_kernel(
+    z_count, arrived_ref, unpack_ref, frozen_ref, first_ref, second_ref, extra_ref,
+    out_ref, fac_ref,
+    part, summed, from_y, from_z, lhs, low,
+    extra_sem, c_send, c_recv, y_send, y_recv, z_send, z_recv,
+):
+    f32, bf16 = jnp.float32, jnp.bfloat16
+    core = lax.axis_index("node")
+    local = lax.axis_index("local")
+    z, y = local // 2, lax.rem(local, 2)
+    tok_rows = out_ref.shape[0]
+    more = fac_ref.shape[0]
+    width = out_ref.shape[1]
+    tile = tile_of(width)
+    nt = (((1,), (1,)), ((), ()))
+    table = visit_order(z_count)
+
+    core_peer = {"node": 1 - core}
+    y_peer = {"local": z * 2 + 1 - y}
+
+    barrier = pltpu.get_barrier_semaphore()
+    pl.semaphore_signal(barrier, inc=1, device_id=core_peer, device_id_type=MESH)
+    pl.semaphore_signal(barrier, inc=1, device_id=y_peer, device_id_type=MESH)
+
+    @pl.when(z > 0)
+    def _():
+        pl.semaphore_signal(barrier, inc=1, device_id={"local": local - 2}, device_id_type=MESH)
+
+    @pl.when(z < z_count - 1)
+    def _():
+        pl.semaphore_signal(barrier, inc=1, device_id={"local": local + 2}, device_id_type=MESH)
+
+    target = []
+    for p in range(z_count):
+        zt = jnp.int32(0)
+        for i in range(z_count):
+            zt = zt + jnp.where(z == i, table[i][p], 0)
+        target.append(zt)
+
+    extra_copies = []
+    for p in range(z_count):
+        copy = pltpu.make_async_copy(
+            extra_ref.at[:, target[p]],
+            part.at[target[p], :, :, pl.ds(tok_rows, more)],
+            extra_sem.at[p],
+        )
+        copy.start()
+        extra_copies.append(copy)
+
+    def compute(p):
+        zt = target[p]
+        for i in range(4):
+            origin = (i // 2) * 2 * z_count + zt * 2 + i % 2
+            rows = jnp.dot(unpack_ref[origin], arrived_ref[origin], preferred_element_type=f32)
+            lhs[pl.ds(i * tok_rows, tok_rows), :] = rows.astype(bf16)
+        low[...] = lax.dot_general(
+            lhs[...], second_ref[...], nt, preferred_element_type=f32
+        ).astype(bf16)
+
+        @pl.loop(0, width // tile)
+        def _(j):
+            columns = pl.ds(pl.multiple_of(j * tile, tile), tile)
+            value = lax.dot_general(
+                lhs[...], frozen_ref[columns, :], nt, preferred_element_type=f32
+            ) + lax.dot_general(low[...], first_ref[columns, :], nt, preferred_element_type=f32)
+            value = value.astype(bf16)
+            for i in range(4):
+                part[zt, i // 2, i % 2, pl.ds(0, tok_rows), columns] = value[
+                    i * tok_rows : (i + 1) * tok_rows
+                ]
+
+        extra_copies[p].wait()
+
+    def c_copy(p):
+        return pltpu.make_async_remote_copy(
+            part.at[target[p], 1 - core], summed.at[target[p]], c_send.at[p], c_recv.at[p],
+            device_id=core_peer, device_id_type=MESH,
+        )
+
+    def y_copy(p):
+        return pltpu.make_async_remote_copy(
+            summed.at[target[p], 1 - y], from_y.at[target[p]], y_send.at[p], y_recv.at[p],
+            device_id=y_peer, device_id_type=MESH,
+        )
+
+    def over_rows(count, step):
+        @pl.loop(0, count // 16)
+        def _(i):
+            step(pl.ds(pl.multiple_of(i * 16, 16), 16))
+
+    def add_core(p):
+        zt = target[p]
+        c_copy(p).wait_recv()
+        for half in (1 - y, y):
+
+            def step(rows):
+                summed[zt, half, rows, :] = (
+                    summed[zt, half, rows, :].astype(f32) + part[zt, core, half, rows, :].astype(f32)
+                ).astype(bf16)
+
+            over_rows(tok_rows + more, step)
+            if half is not y:
+                y_copy(p).start()
+
+    compute(0)
+    neighbours = 2 + jnp.where(z > 0, 1, 0) + jnp.where(z < z_count - 1, 1, 0)
+    pl.semaphore_wait(barrier, neighbours)
+    c_copy(0).start()
+    for p in range(1, z_count):
+        compute(p)
+        c_copy(p).start()
+        add_core(p - 1)
+    add_core(z_count - 1)
+
+    def z_copy(p, slot, peer):
+        return pltpu.make_async_remote_copy(
+            summed.at[target[p], y], from_z.at[slot], z_send.at[p], z_recv.at[slot],
+            device_id={"local": peer}, device_id_type=MESH,
+        )
+
+    def slot_wait(slot):
+        z_copy(0, slot, local).wait_recv()
+
+    for p in range(z_count - 1):
+        zt = target[p]
+        up = zt > z
+        y_copy(p).wait_recv()
+        passing = jnp.logical_or(jnp.logical_and(up, z > 0), jnp.logical_and(zt < z, z < z_count - 1))
+
+        @pl.when(passing)
+        def _():
+            slot_wait(zt)
+
+            def step(rows):
+                summed[zt, y, rows, :] = (
+                    summed[zt, y, rows, :].astype(f32)
+                    + from_y[zt, rows, :].astype(f32)
+                    + from_z[zt, rows, :].astype(f32)
+                ).astype(bf16)
+
+            over_rows(tok_rows + more, step)
+
+        @pl.when(jnp.logical_not(passing))
+        def _():
+            def step(rows):
+                summed[zt, y, rows, :] = (
+                    summed[zt, y, rows, :].astype(f32) + from_y[zt, rows, :].astype(f32)
+                ).astype(bf16)
+
+            over_rows(tok_rows + more, step)
+
+        slot = jnp.where(zt == z - 1, z_count, zt)
+        z_copy(p, slot, jnp.where(up, local + 2, local - 2)).start()
+
+    p = z_count - 1
+    y_copy(p).wait_recv()
+
+    def finish(with_below, with_above):
+        def total(rows):
+            value = summed[z, y, rows, :].astype(f32) + from_y[z, rows, :].astype(f32)
+            if with_below:
+                value = value + from_z[z, rows, :].astype(f32)
+            if with_above:
+                value = value + from_z[z_count, rows, :].astype(f32)
+            return value
+
+        if with_below:
+            slot_wait(z)
+        if with_above:
+            slot_wait(z_count)
+
+        def step(rows):
+            out_ref[rows, :] = total(rows).astype(bf16)
+
+        over_rows(tok_rows, step)
+        for start in range(0, more, 16):
+            fac_ref[pl.ds(start, 16), :] = total(pl.ds(tok_rows + start, 16))
+
+    @pl.when(z == 0)
+    def _():
+        finish(False, True)
+
+    @pl.when(z == z_count - 1)
+    def _():
+        finish(True, False)
+
+    @pl.when(jnp.logical_and(z > 0, z < z_count - 1))
+    def _():
+        finish(True, True)
+
+    for p in range(z_count):
+        c_copy(p).wait_send()
+        y_copy(p).wait_send()
+    for p in range(z_count - 1):
+        z_copy(p, 0, local).wait_send()
+
+
+def return_sums(arrived, unpack, frozen, first, second, extra, tok_rows):
+    bf16 = jnp.bfloat16
+    z_count, more, width = extra.shape[1], extra.shape[3], extra.shape[4]
+    rows = tok_rows + more
+    dma = pltpu.SemaphoreType.DMA
+    vmem = pl.BlockSpec(memory_space=pltpu.VMEM)
+    routes = 4 * z_count * tok_rows
+    return pl.pallas_call(
+        functools.partial(return_kernel, z_count),
+        out_shape=(
+            jax.ShapeDtypeStruct((tok_rows, width), bf16),
+            jax.ShapeDtypeStruct((more, width), jnp.float32),
+        ),
+        in_specs=[vmem] * 5 + [pl.BlockSpec(memory_space=pl.ANY)],
+        out_specs=(vmem, vmem),
+        scratch_shapes=[
+            pltpu.VMEM((z_count, 2, 2, rows, width), bf16),
+            pltpu.VMEM((z_count, 2, rows, width), bf16),
+            pltpu.VMEM((z_count, rows, width), bf16),
+            pltpu.VMEM((z_count + 1, rows, width), bf16),
+            pltpu.VMEM((4 * tok_rows, frozen.shape[1]), bf16),
+            pltpu.VMEM((4 * tok_rows, second.shape[0]), bf16),
+            dma((z_count,)), dma((z_count,)), dma((z_count,)), dma((z_count,)),
+            dma((z_count,)), dma((z_count,)), dma((z_count + 1,)),
+        ],
+        compiler_params=pltpu.CompilerParams(
+            collective_id=0, has_side_effects=True, vmem_limit_bytes=60 * 2**20
+        ),
+        cost_estimate=pl.CostEstimate(
+            flops=2 * routes * width * frozen.shape[1], bytes_accessed=20 * 2**20, transcendentals=0
+        ),
+    )(arrived, unpack, frozen, first, second, extra)
+
+
 def scale_routes(grads, route_weights):
     pair_count = grads.shape[0] * grads.shape[1]
     return (
@@ -180,32 +438,27 @@
     ).reshape(tok_rows * topk, -1)
     share_a = lax.dot_general(middle, tokens, (((0,), (0,)), ((), ())), preferred_element_type=f32)
     share_b = lax.dot_general(projected, scaled, (((0,), (0,)), ((), ())), preferred_element_type=f32)
-    shares = jnp.concatenate([share_a.astype(bf16), share_b.astype(bf16)], axis=1)
-    factor_gradients = lax.psum_scatter(shares, "node", scatter_dimension=0, tiled=True)
-    factor_gradients = lax.psum_scatter(factor_gradients, "local", scatter_dimension=0, tiled=True)
-    factor_gradients = factor_gradients.astype(f32) * (weight_gradient_total * adapter_scale_factor)
+    half = rank // 2
+    share_b = share_b.astype(bf16).reshape(device_count, 2, half, hidden)
+    share_b = jnp.concatenate([share_b[:, 0], share_b[:, 1]], axis=2)
+    share_b = jnp.pad(share_b, ((0, 0), (0, 0), (0, width - 2 * hidden)))
+    extra = jnp.concatenate(
+        [share_a.astype(bf16).reshape(device_count, rank, width), share_b], axis=1
+    ).reshape(2, device_count // 4, 2, rank + half, width)
 
     mine = (tables == me.astype(bf16)).any(axis=1)
     place = jnp.cumsum(mine.astype(jnp.int32), axis=1) - 1
     unpack = (
         mine[:, :, None] & (place[:, :, None] == jnp.arange(slot_most, dtype=jnp.int32))
     ).astype(bf16)
-    rows = (
-        lax.dot_general(unpack, arrived, (((2,), (1,)), ((0,), (0,))), preferred_element_type=f32)
-        .astype(bf16)
-        .reshape(device_count * tok_rows, hidden)
-    )
-    row_middle = lax.dot_general(
-        rows, second, (((1,), (1,)), ((), ())), preferred_element_type=f32
-    ).astype(bf16)
-    joined_rows = jnp.concatenate([rows, row_middle], axis=1)
-    joined_weight = jnp.concatenate([frozen_up[0], factor_a[0] * adapter_scale_factor], axis=1)
-    partial = lax.dot_general(
-        joined_rows, joined_weight, (((1,), (1,)), ((), ())), preferred_element_type=f32
-    ).astype(bf16)
-    partial = lax.psum_scatter(partial, "node", scatter_dimension=0, tiled=True)
-    input_grad = lax.psum_scatter(partial, "local", scatter_dimension=0, tiled=True)
-    return (input_grad, factor_gradients[:, :width].T[None], factor_gradients[:, width:][None])
+    input_grad, factor_sums = return_sums(
+        arrived, unpack, frozen_up[0], factor_a[0] * adapter_scale_factor, second, extra, tok_rows
+    )
+    factor_sums = factor_sums * (weight_gradient_total * adapter_scale_factor)
+    grad_a = factor_sums[:rank].T[None]
+    last = factor_sums[rank:]
+    grad_b = jnp.concatenate([last[:, :hidden], last[:, hidden : 2 * hidden]], axis=0)[None]
+    return (input_grad, grad_a, grad_b)
 
 
 def body(tokens, grads, route_weights, route_ids, group_picks, frozen_up, factor_a, factor_b):

time: 420 us -> 262 us (0.62)
  waiting for transfers between devices: 336 us -> 67.9 us
  Pallas kernels: 0 us -> 141 us
  matrix products: 43 us -> 14.3 us
    reduce_scatter x4 -> x0, waiting for transfers between devices: 229 us -> none  [the longest x1 133 us: dense_body(): lax.psum_scatter(partial, 'local', scatter_dimension=0, tiled=True)]
    pallas_call x0 -> x1, Pallas kernels: none -> 141 us  [return_sums(): pl.pallas_call(functools.partial(return_kernel, z_count), out_shape=(jax....]
    all_to_all x1, waiting for transfers between devices: 53.9 us -> 0.55 us  [dense_body(): lax.all_to_all(send_g.reshape(device_count, slot_most, hidden), axes, spl...]
    dot_general x3 -> x0, matrix products: 28.9 us -> none  [the longest x1 25.5 us: dense_body(): lax.dot_general(joined_rows, joined_weight, (((1,), (1,)), ((), ())), pre...]
    all_gather x1, waiting for transfers between devices: 52.2 us -> 67.3 us  [dense_body(): lax.all_gather(jnp.concatenate([first_t, second, table], axis=1), axes, a...]
  transfers between devices with their start and end apart: 6 -> 2, of which waited for: 5 -> 2; matrix products, arithmetic and copies ran while one was open for 11% -> 10% of each run, Pallas kernels for 0% -> 0%
where the time goes in v2:
time: 262 us
  Pallas kernels  141 us (54%)
  waiting for transfers between devices  67.9 us (26%)
  matrix products  14.3 us (5%)
  between operations  14.2 us (5%)
  other arithmetic  13 us (5%)
  starting transfers between devices  6.46 us (2%)
  local copies, waits for them, and re-layouts  4.64 us (2%)
    pallas_call x1, Pallas kernels, return_sums(): pl.pallas_call(functools.partial(return_kernel, z_count), out_shape=(jax....  141 us
    all_gather x1, waiting for transfers between devices, dense_body(): lax.all_gather(jnp.concatenate([first_t, second, table], axis=1), axes, a...  67.3 us
    all_to_all x1, starting transfers between devices, dense_body(): lax.all_to_all(send_g.reshape(device_count, slot_most, hidden), axes, spl...  6.43 us
  transfers between devices with their start and end apart: 2, of which 2 were waited for; matrix products, arithmetic and copies ran while one was open for 10% of the time, Pallas kernels for 0%

profile of v2, /device:TPU:8, one launch (start us, length us, event | category | flops | bytes accessed | tf_op | source)
XLA Modules:
  0.0 261.7 jit_solution(13377661544438633484)
XLA Ops:
  7.2 0.0 copy-start
  7.2 0.0 all-gather.2.cloned.1.call-start
  7.2 0.8 broadcast_multiply_fusion.1
  8.0 0.7 convert_bitcast_fusion
  8.7 1.7 fusion.31
  10.4 0.0 all-gather.2.cloned.1.call-update
  10.4 0.1 copy.39
  10.5 0.2 reduce_window_sum.22
  10.7 0.1 copy.40
  10.8 0.1 copy.41
  10.9 0.1 eq.83
  11.0 0.8 copy.42
  11.8 2.0 multiply_convert_fusion
  13.8 0.0 copy-start.1
  13.8 4.2 %fusion.1 = bf16[1280,1024]{1,0:T(8,128)(2,1)} fusion(s32[1024]{0:T(1024)S(1)} %eq.83, bf16[128,8,1024]{2,1,0:T(8,128)(2,1)S(1)} %multiply_convert_fusion), kind=kOutput, calls=%fused_computation.5 | convolution fusion | flops 2686976000 | bytes 4722688 | tf_op jit(solution)/shard_map/dot_general | solution.py:425
  18.0 0.0 copy-done.1
  18.0 0.0 copy-start.4
  18.0 6.4 %all-to-all-start = ((bf16[16,80,1024]{2,1,0:T(8,128)(2,1)}), bf16[16,80,1024]{2,1,0:T(8,128)(2,1)}, u32[]{:S(2)}, u32[]{:S(2)}) async-start(bf16[16,80,1024]{2,1,0:T(8,128)(2,1)} %bitcast.2), calls=%async_computation | async-start | bytes 5242880 | tf_op jit(solution)/shard_map/all_to_all | solution.py:426
  24.4 0.1 copy.45
  24.5 0.0 copy-done.4
  24.5 0.5 copy.43
  25.0 0.1 eq.94
  25.1 0.1 eq.92
  25.2 1.0 bitcast_multiply_fusion.first_ref
  26.2 67.3 %all-gather.2.cloned.1.call-done = bf16[512,4736]{1,0:T(8,128)(2,1)} async-done(((bf16[32,4736]{1,0:T(8,128)(2,1)}), bf16[512,4736]{1,0:T(8,128)(2,1)}) %all-gather.2.cloned.1.call-update) | async-done | bytes 4849680 | tf_op jit(solution)/shard_map/all_gather | solution.py:410
  93.5 0.9 slice.55
  94.5 0.3 reduce_window_sum.23
  94.8 1.4 fusion.27.unpack_ref
  96.2 0.0 copy-done
  96.2 0.0 copy-start.2
  96.2 3.3 %fusion.20 = bf16[128,512]{0,1:T(8,128)(2,1)S(1)} fusion(bf16[128,3584]{1,0:T(8,128)(2,1)S(1)} %copy-done, bf16[512,4736]{1,0:T(8,128)(2,1)} %all-gather.2.cloned.1.call-done), kind=kOutput, calls=%fused_computation.22 | convolution fusion | flops 469827584 | bytes 4718592 | tf_op jit(solution)/shard_map/dot_general | solution.py:433
  99.5 0.0 copy-done.2
  99.5 2.8 %bitcast_convert_fusion = bf16[512,1024]{1,0:T(8,128)(2,1)S(1)} fusion(bf16[128,8,1024]{2,1,0:T(8,128)(2,1)S(1)} %copy-done.2, s32[128,8]{0,1:T(8,128)S(1)} %get-tuple-element.20, s32[512]{0:T(512)S(1)} %eq.94, bf16[128,512]{0,1:T(8,128)(2,1)S(1)} %fusion.20), kind=kOutput, calls=%fused_computation.12 | convolution fusion | flops 1075314688 | bytes 3282944 | tf_op jit(solution)/shard_map/dot_general | solution.py:440
  102.3 0.1 slice_bitcast_fusion.1
  102.4 2.9 %bitcast_reduce_fusion = bf16[128,512]{1,0:T(8,128)(2,1)S(1)} fusion(bf16[128,8,1024]{2,1,0:T(8,128)(2,1)S(1)} %copy-done.2, bf16[512,4736]{1,0:T(8,128)(2,1)} %all-gather.2.cloned.1.call-done, s32[512]{0:T(512)S(1)} %eq.94, s32[1024]{0:T(1024)S(1)} %eq.92), kind=kOutput, calls=%fused_computation.13 | convolution fusion | flops 1075249152 | bytes 3282944 | tf_op jit(solution)/shard_map/dot_general | solution.py:431
  105.4 1.1 convolution_convert_fusion
  106.5 0.2 fusion.12
  106.7 2.7 %pad_maximum_fusion.extra_ref = bf16[2,4,2,48,3584]{4,3,2,1,0:T(8,128)(2,1)} fusion(bf16[2,4,2,16,3584]{4,3,2,1,0:T(8,128)(2,1)S(1)} %bitcast.45, bf16[2,4,2,32,3584]{4,3,2,1,0:T(8,128)(2,1)S(1)} %bitcast.44), kind=kLoop, calls=%fused_computation.1 | loop fusion | flops 11010048 | bytes 11010048 | tf_op jit(solution)/shard_map/concatenate | solution.py:445
  109.4 0.5 all-to-all-done.arrived_ref
  110.0 141.3 %shard_map.103 = (bf16[128,3584]{1,0:T(8,128)(2,1)}, f32[48,3584]{1,0:T(8,128)}) custom-call(bf16[16,80,1024]{2,1,0:T(8,128)(2,1)} %all-to-all-done.arrived_ref, bf16[16,128,80]{2,1,0:T(8,128)(2,1)} %fusion.27.unpack_ref, bf16[3584,1024]{1,0:T(8,128)(2,1)} %bitcast.52, bf16[3584,32]{1,0:T(8,128)(2,1)} %bitcast_multiply_fusion.first_ref, ...), custom_call_target="tpu_custom_call" | custom-call | flops 15032385536 | bytes 20971520 | tf_op jit(solution)/shard_map/pallas_call | solution.py:358
  251.2 0.0 copy-start.3
  251.3 1.2 broadcast_multiply_fusion
  252.5 0.8 slice_bitcast_fusion.2
  253.3 0.7 maximum_bitcast_fusion
  254.0 0.0 copy-done.3
  254.0 0.9 copy.57
  (11 shorter events, 0.1 us)
Async XLA Ops:
  7.2 89.0 %copy-start = (bf16[128,3584]{1,0:T(8,128)(2,1)S(1)}, bf16[128,3584]{1,0:T(8,128)(2,1)}, u32[]{:S(2)}) copy-start(bf16[128,3584]{1,0:T(8,128)(2,1)} %param.10) | copy-start | bytes 2752516
  7.2 86.3 %all-gather.2.cloned.1.call-start = ((), (), s32[]{:S(2)}) async-start(), calls=%async_computation.1 | async-start | bytes 5152768 | tf_op jit(solution)/shard_map/all_gather | solution.py:410
  13.8 4.2 %copy-start.1 = (bf16[128,8,1024]{2,1,0:T(8,128)(2,1)}, bf16[128,8,1024]{2,1,0:T(8,128)(2,1)S(1)}, u32[]{:S(2)}) copy-start(bf16[128,8,1024]{2,1,0:T(8,128)(2,1)S(1)} %multiply_convert_fusion) | copy-start | bytes 6291460
  18.0 6.5 %copy-start.4 = (bf16[1,3584,32]{1,2,0:T(8,128)(2,1)S(1)}, bf16[1,3584,32]{1,2,0:T(8,128)(2,1)}, u32[]{:S(2)}) copy-start(bf16[1,3584,32]{1,2,0:T(8,128)(2,1)} %param.16) | copy-start | bytes 688132
  18.0 92.0 %all-to-all-start = ((bf16[16,80,1024]{2,1,0:T(8,128)(2,1)}), bf16[16,80,1024]{2,1,0:T(8,128)(2,1)}, u32[]{:S(2)}, u32[]{:S(2)}) async-start(bf16[16,80,1024]{2,1,0:T(8,128)(2,1)} %bitcast.2), calls=%async_computation | async-start | bytes 5242880 | tf_op jit(solution)/shard_map/all_to_all | solution.py:426
  96.2 3.3 %copy-start.2 = (bf16[128,8,1024]{2,1,0:T(8,128)(2,1)S(1)}, bf16[128,8,1024]{2,1,0:T(8,128)(2,1)}, u32[]{:S(2)}) copy-start(bf16[128,8,1024]{2,1,0:T(8,128)(2,1)} %copy-done.1) | copy-start | bytes 6291460
  251.2 2.7 %copy-start.3 = (bf16[128,3584]{1,0:T(8,128)(2,1)S(1)}, bf16[128,3584]{1,0:T(8,128)(2,1)}, u32[]{:S(2)}) copy-start(bf16[128,3584]{1,0:T(8,128)(2,1)} %get-tuple-element.28) | copy-start | bytes 2752516
Sparse Core Ops, SparseCore 0:
  10.8 82.6 all-gather.1

commit v3 on v2

--- a/solution.py
+++ b/solution.py
@@ -382,6 +382,133 @@
     )(arrived, unpack, frozen, first, second, extra)
 
 
+def gather_kernel(z_count, own_ref, all_ref, own_sem, recv, up_send, down_send, y_send, c_send):
+    core = lax.axis_index("node")
+    local = lax.axis_index("local")
+    z, y = local // 2, lax.rem(local, 2)
+    core_peer = {"node": 1 - core}
+    y_peer = {"local": z * 2 + 1 - y}
+    above, below = {"local": local + 2}, {"local": local - 2}
+    has_above, has_below = z < z_count - 1, z > 0
+
+    barrier = pltpu.get_barrier_semaphore()
+    pl.semaphore_signal(barrier, inc=1, device_id=core_peer, device_id_type=MESH)
+    pl.semaphore_signal(barrier, inc=1, device_id=y_peer, device_id_type=MESH)
+
+    @pl.when(has_below)
+    def _():
+        pl.semaphore_signal(barrier, inc=1, device_id=below, device_id_type=MESH)
+
+    @pl.when(has_above)
+    def _():
+        pl.semaphore_signal(barrier, inc=1, device_id=above, device_id_type=MESH)
+
+    place = pltpu.make_async_copy(own_ref, all_ref.at[core, z, y], own_sem)
+    place.start()
+    place.wait()
+    neighbours = 2 + jnp.where(has_below, 1, 0) + jnp.where(has_above, 1, 0)
+    pl.semaphore_wait(barrier, neighbours)
+
+    def copy(zs, ys, send_sem, peer):
+        return pltpu.make_async_remote_copy(
+            all_ref.at[core, zs, ys], all_ref.at[core, zs, ys], send_sem, recv.at[core, zs, ys],
+            device_id=peer, device_id_type=MESH,
+        )
+
+    def arrival(cs, zs, ys):
+        pltpu.make_async_remote_copy(
+            all_ref.at[cs, zs, ys], all_ref.at[cs, zs, ys], own_sem, recv.at[cs, zs, ys],
+            device_id=core_peer, device_id_type=MESH,
+        ).wait_recv()
+
+    def spread(zs):
+        copy(zs, y, y_send.at[zs], y_peer).start()
+        copy(zs, y, c_send.at[zs, y], core_peer).start()
+
+    @pl.when(has_above)
+    def _():
+        copy(z, y, up_send.at[z], above).start()
+
+    @pl.when(has_below)
+    def _():
+        copy(z, y, down_send.at[z], below).start()
+
+    spread(z)
+    for distance in range(1, z_count):
+
+        @pl.when(z - distance >= 0)
+        def _():
+            zs = z - distance
+            arrival(core, zs, y)
+
+            @pl.when(has_above)
+            def _():
+                copy(zs, y, up_send.at[zs], above).start()
+
+            spread(zs)
+
+        @pl.when(z + distance < z_count)
+        def _():
+            zs = z + distance
+            arrival(core, zs, y)
+
+            @pl.when(has_below)
+            def _():
+                copy(zs, y, down_send.at[zs], below).start()
+
+            spread(zs)
+
+    def from_y(zs):
+        arrival(core, zs, 1 - y)
+        copy(zs, 1 - y, c_send.at[zs, 1 - y], core_peer).start()
+
+    from_y(z)
+    for distance in range(1, z_count):
+
+        @pl.when(z - distance >= 0)
+        def _():
+            from_y(z - distance)
+
+        @pl.when(z + distance < z_count)
+        def _():
+            from_y(z + distance)
+
+    for zs in range(z_count):
+        for ys in range(2):
+            arrival(1 - core, zs, ys)
+            copy(zs, ys, c_send.at[zs, ys], core_peer).wait_send()
+        copy(zs, y, y_send.at[zs], y_peer).wait_send()
+
+        @pl.when(jnp.logical_and(has_above, zs <= z))
+        def _():
+            copy(zs, y, up_send.at[zs], core_peer).wait_send()
+
+        @pl.when(jnp.logical_and(has_below, zs >= z))
+        def _():
+            copy(zs, y, down_send.at[zs], core_peer).wait_send()
+
+
+def gather_shards(own, device_count):
+    z_count = device_count // 4
+    dma = pltpu.SemaphoreType.DMA
+    vmem = pl.BlockSpec(memory_space=pltpu.VMEM)
+    gathered = pl.pallas_call(
+        functools.partial(gather_kernel, z_count),
+        out_shape=jax.ShapeDtypeStruct((2, z_count, 2) + own.shape, own.dtype),
+        in_specs=[vmem],
+        out_specs=vmem,
+        scratch_shapes=[
+            dma, dma((2, z_count, 2)), dma((z_count,)), dma((z_count,)),
+            dma((z_count,)), dma((z_count, 2)),
+        ],
+        compiler_params=pltpu.CompilerParams(
+            collective_id=1, has_side_effects=True, vmem_limit_bytes=24 * 2**20
+        ),
+        cost_estimate=pl.CostEstimate(flops=0, bytes_accessed=100 * 2**20, transcendentals=0),
+    )(own)
+    return gathered.reshape((device_count * own.shape[0],) + own.shape[1:])
+
+
 def scale_routes(grads, route_weights):
     pair_count = grads.shape[0] * grads.shape[1]
     return (
@@ -407,13 +534,6 @@
     first_t = factor_a[0].T
     second = factor_b[0]
     table = jnp.zeros((rank, tok_rows), bf16).at[:topk].set(experts.T.astype(bf16))
-    shared = lax.all_gather(
-        jnp.concatenate([first_t, second, table], axis=1), axes, axis=0, tiled=True
-    )
-    all_first = shared[:, :width]
-    all_second = shared[:, width : width + hidden]
-    tables = shared[:, width + hidden :].reshape(device_count, rank, tok_rows)[:, :topk]
-
     ids = jnp.arange(device_count, dtype=jnp.int32)
     member = (experts[:, :, None] == ids[None, None, :]).any(axis=1)
     order = jnp.cumsum(member.astype(jnp.int32), axis=0) - 1
@@ -423,9 +543,16 @@
     slots = jnp.arange(device_count * slot_most, dtype=jnp.int32)
     pack = (target.reshape(1, -1) == slots[:, None]).astype(bf16)
     send_g = jnp.dot(pack, scaled, preferred_element_type=f32).astype(bf16)
+    own = jnp.concatenate([first_t, second, table], axis=1)
+    own, send_g = lax.optimization_barrier((own, send_g))
     arrived = lax.all_to_all(
         send_g.reshape(device_count, slot_most, hidden), axes, split_axis=0, concat_axis=0, tiled=True
     )
+
+    shared = gather_shards(own, device_count)
+    all_first = shared[:, :width]
+    all_second = shared[:, width : width + hidden]
+    tables = shared[:, width + hidden :].reshape(device_count, rank, tok_rows)[:, :topk]
 
     owner_mask = expert_flat[:, None] == jnp.repeat(ids, rank)[None, :]
     middle = lax.dot_general(scaled, all_second, (((1,), (1,)), ((), ())), preferred_element_type=f32)

time: 262 us -> 264 us (level)
  Pallas kernels: 141 us -> 225 us
  waiting for transfers between devices: 67.9 us -> 0.01 us
  between operations: 14.2 us -> 0.85 us
    pallas_call x0 -> x1, Pallas kernels: none -> 83.2 us  [gather_shards(): pl.pallas_call(functools.partial(gather_kernel, z_count), out_shape=jax.S...]
    all_gather x1 -> x0, waiting for transfers between devices: 67.3 us -> none  [dense_body(): lax.all_gather(jnp.concatenate([first_t, second, table], axis=1), axes, a...]
  transfers between devices with their start and end apart: 2 -> 1, of which waited for: 2 -> 0; matrix products, arithmetic and copies ran while one was open for 10% -> 6% of each run, Pallas kernels for 0% -> 32%
where the time goes in v3:
time: 264 us; the launch traced here: 263 us
  Pallas kernels  225 us (85%)
  matrix products  14.4 us (5%)
  other arithmetic  11.3 us (4%)
  starting transfers between devices  6.31 us (2%)
  local copies, waits for them, and re-layouts  5.83 us (2%)
    pallas_call x1, Pallas kernels, return_sums(): pl.pallas_call(functools.partial(return_kernel, z_count), out_shape=(jax....  142 us
    pallas_call x1, Pallas kernels, gather_shards(): pl.pallas_call(functools.partial(gather_kernel, z_count), out_shape=jax.S...  83.2 us
    all_to_all x1, starting transfers between devices, dense_body(): lax.all_to_all(send_g.reshape(device_count, slot_most, hidden), axes, spl...  6.31 us
  transfers between devices with their start and end apart: 1, of which 0 were waited for; matrix products, arithmetic and copies ran while one was open for 6% of the time, Pallas kernels for 32%

profile of v3, /device:TPU:8, one launch (start us, length us, event | category | flops | bytes accessed | tf_op | source)
XLA Modules:
  0.0 263.5 jit_solution(6126475724886218220)
XLA Ops:
  0.6 0.0 copy-start
  0.6 0.8 broadcast_multiply_fusion.1
  1.4 0.7 convert_bitcast_fusion
  2.1 0.1 copy.42
  2.2 0.2 reduce_window_sum.22
  2.4 0.1 copy.43
  2.5 0.1 copy.44
  2.6 0.1 eq.83
  2.7 0.8 copy.45
  3.5 2.0 multiply_convert_fusion
  5.5 0.0 copy-start.2
  5.5 0.0 copy-start.5
  5.5 0.0 copy-start.6
  5.5 4.2 %fusion.1 = bf16[1280,1024]{1,0:T(8,128)(2,1)} fusion(s32[1024]{0:T(1024)S(1)} %eq.83, bf16[128,8,1024]{2,1,0:T(8,128)(2,1)S(1)} %multiply_convert_fusion), kind=kOutput, calls=%fused_computation.5 | convolution fusion | flops 2686976000 | bytes 4722688 | tf_op jit(solution)/shard_map/dot_general | solution.py:545
  9.8 0.0 copy-done.2
  9.8 0.0 copy-done.5
  9.8 0.0 copy-done.6
  9.8 6.3 %all-to-all-start = ((bf16[16,80,1024]{2,1,0:T(8,128)(2,1)}), bf16[16,80,1024]{2,1,0:T(8,128)(2,1)}, u32[]{:S(2)}, u32[]{:S(2)}) async-start(bf16[16,80,1024]{2,1,0:T(8,128)(2,1)} %bitcast.50), calls=%async_computation | async-start | bytes 5242880 | tf_op jit(solution)/shard_map/all_to_all | solution.py:548
  16.1 0.1 copy.46
  16.2 0.4 copy.40
  16.7 0.1 eq.94
  16.7 0.1 eq.92
  16.8 83.2 %shard_map.103 = bf16[2,4,2,32,4736]{4,3,2,1,0:T(8,128)(2,1)S(1)} custom-call(bf16[32,4736]{1,0:T(8,128)(2,1)S(1)} %fusion.31.own_ref), custom_call_target="tpu_custom_call" | custom-call | bytes 104857600 | tf_op jit(solution)/shard_map/pallas_call | solution.py:495
  100.1 0.0 copy-start.1
  100.1 2.1 copy-done.1
  102.3 0.3 reduce_window_sum.23
  102.6 1.4 fusion.27.unpack_ref
  104.0 0.0 copy-done
  104.0 0.0 copy-start.3
  104.0 3.3 %fusion.20 = bf16[128,512]{0,1:T(8,128)(2,1)S(1)} fusion(bf16[128,3584]{1,0:T(8,128)(2,1)S(1)} %copy-done, bf16[512,4736]{1,0:T(8,128)(2,1)} %bitcast.46), kind=kOutput, calls=%fused_computation.22 | convolution fusion | flops 469827584 | bytes 4718592 | tf_op jit(solution)/shard_map/dot_general | solution.py:560
  107.3 0.0 copy-done.3
  107.3 2.8 %bitcast_convert_fusion = bf16[512,1024]{1,0:T(8,128)(2,1)S(1)} fusion(bf16[128,8,1024]{2,1,0:T(8,128)(2,1)S(1)} %copy-done.3, s32[128,8]{0,1:T(8,128)S(1)} %get-tuple-element.24, s32[512]{0:T(512)S(1)} %eq.94, bf16[128,512]{0,1:T(8,128)(2,1)S(1)} %fusion.20), kind=kOutput, calls=%fused_computation.12 | convolution fusion | flops 1075314688 | bytes 3282944 | tf_op jit(solution)/shard_map/dot_general | solution.py:567
  110.1 0.1 slice_bitcast_fusion.1
  110.2 2.9 %bitcast_reduce_fusion = bf16[128,512]{1,0:T(8,128)(2,1)S(1)} fusion(bf16[128,8,1024]{2,1,0:T(8,128)(2,1)S(1)} %copy-done.3, bf16[512,4736]{1,0:T(8,128)(2,1)} %bitcast.47, s32[512]{0:T(512)S(1)} %eq.94, s32[1024]{0:T(1024)S(1)} %eq.92), kind=kOutput, calls=%fused_computation.13 | convolution fusion | flops 1075249152 | bytes 3282944 | tf_op jit(solution)/shard_map/dot_general | solution.py:558
  113.1 1.1 convolution_convert_fusion
  114.3 0.2 fusion.12
  114.4 2.8 %pad_maximum_fusion.extra_ref = bf16[2,4,2,48,3584]{4,3,2,1,0:T(8,128)(2,1)} fusion(bf16[2,4,2,16,3584]{4,3,2,1,0:T(8,128)(2,1)S(1)} %bitcast.49, bf16[2,4,2,32,3584]{4,3,2,1,0:T(8,128)(2,1)S(1)} %bitcast.48), kind=kLoop, calls=%fused_computation.1 | loop fusion | flops 11010048 | bytes 11010048 | tf_op jit(solution)/shard_map/concatenate | solution.py:572
  117.2 1.0 bitcast_multiply_fusion.first_ref
  118.3 0.0 all-to-all-done.arrived_ref
  118.3 141.6 %shard_map.104 = (bf16[128,3584]{1,0:T(8,128)(2,1)}, f32[48,3584]{1,0:T(8,128)}) custom-call(bf16[16,80,1024]{2,1,0:T(8,128)(2,1)} %all-to-all-done.arrived_ref, bf16[16,128,80]{2,1,0:T(8,128)(2,1)} %fusion.27.unpack_ref, bf16[3584,1024]{1,0:T(8,128)(2,1)} %bitcast.57, bf16[3584,32]{1,0:T(8,128)(2,1)} %bitcast_multiply_fusion.first_ref, ...), custom_call_target="tpu_custom_call" | custom-call | flops 15032385536 | bytes 20971520 | tf_op jit(solution)/shard_map/pallas_call | solution.py:358
  259.8 0.0 copy-start.4
  259.8 1.2 broadcast_multiply_fusion
  261.1 0.8 slice_bitcast_fusion.2
  261.9 0.7 maximum_bitcast_fusion
  262.6 0.0 copy-done.4
  262.6 0.9 copy.58
  (13 shorter events, 0.2 us)
Async XLA Ops:
  0.6 103.4 %copy-start = (bf16[128,3584]{1,0:T(8,128)(2,1)S(1)}, bf16[128,3584]{1,0:T(8,128)(2,1)}, u32[]{:S(2)}) copy-start(bf16[128,3584]{1,0:T(8,128)(2,1)} %param.10) | copy-start | bytes 2752516
  5.5 4.2 %copy-start.2 = (bf16[128,8,1024]{2,1,0:T(8,128)(2,1)}, bf16[128,8,1024]{2,1,0:T(8,128)(2,1)S(1)}, u32[]{:S(2)}) copy-start(bf16[128,8,1024]{2,1,0:T(8,128)(2,1)S(1)} %multiply_convert_fusion) | copy-start | bytes 6291460
  5.5 4.2 %copy-start.5 = (bf16[1,3584,32]{1,2,0:T(8,128)(2,1)S(1)}, bf16[1,3584,32]{1,2,0:T(8,128)(2,1)}, u32[]{:S(2)}) copy-start(bf16[1,3584,32]{1,2,0:T(8,128)(2,1)} %param.16) | copy-start | bytes 688132
  5.5 4.2 %copy-start.6 = (bf16[1,32,1024]{2,1,0:T(8,128)(2,1)S(1)}, bf16[1,32,1024]{2,1,0:T(8,128)(2,1)}, u32[]{:S(2)}) copy-start(bf16[1,32,1024]{2,1,0:T(8,128)(2,1)} %param.17) | copy-start | bytes 196612
  9.8 108.5 %all-to-all-start = ((bf16[16,80,1024]{2,1,0:T(8,128)(2,1)}), bf16[16,80,1024]{2,1,0:T(8,128)(2,1)}, u32[]{:S(2)}, u32[]{:S(2)}) async-start(bf16[16,80,1024]{2,1,0:T(8,128)(2,1)} %bitcast.50), calls=%async_computation | async-start | bytes 5242880 | tf_op jit(solution)/shard_map/all_to_all | solution.py:548
  100.1 2.2 copy-start.1
  104.0 3.3 %copy-start.3 = (bf16[128,8,1024]{2,1,0:T(8,128)(2,1)S(1)}, bf16[128,8,1024]{2,1,0:T(8,128)(2,1)}, u32[]{:S(2)}) copy-start(bf16[128,8,1024]{2,1,0:T(8,128)(2,1)} %copy-done.2) | copy-start | bytes 6291460
  259.8 2.7 %copy-start.4 = (bf16[128,3584]{1,0:T(8,128)(2,1)S(1)}, bf16[128,3584]{1,0:T(8,128)(2,1)}, u32[]{:S(2)}) copy-start(bf16[128,3584]{1,0:T(8,128)(2,1)} %get-tuple-element.32) | copy-start | bytes 2752516

commit v4 on v3

--- a/solution.py
+++ b/solution.py
@@ -152,10 +152,10 @@
 
 
 def return_kernel(
-    z_count, arrived_ref, unpack_ref, frozen_ref, first_ref, second_ref, extra_ref,
+    z_count, send_ref, unpack_ref, frozen_ref, first_ref, second_ref, extra_ref,
     out_ref, fac_ref,
-    part, summed, from_y, from_z, lhs, low,
-    extra_sem, c_send, c_recv, y_send, y_recv, z_send, z_recv,
+    arrived, part, summed, from_y, from_z, lhs, low,
+    a_send, a_recv, extra_sem, c_send, c_recv, y_send, y_recv, z_send, z_recv,
 ):
     f32, bf16 = jnp.float32, jnp.bfloat16
     core = lax.axis_index("node")
@@ -171,17 +171,15 @@
     core_peer = {"node": 1 - core}
     y_peer = {"local": z * 2 + 1 - y}
 
+    device_count = 4 * z_count
+    me = core * 2 * z_count + local
     barrier = pltpu.get_barrier_semaphore()
-    pl.semaphore_signal(barrier, inc=1, device_id=core_peer, device_id_type=MESH)
-    pl.semaphore_signal(barrier, inc=1, device_id=y_peer, device_id_type=MESH)
-
-    @pl.when(z > 0)
-    def _():
-        pl.semaphore_signal(barrier, inc=1, device_id={"local": local - 2}, device_id_type=MESH)
-
-    @pl.when(z < z_count - 1)
-    def _():
-        pl.semaphore_signal(barrier, inc=1, device_id={"local": local + 2}, device_id_type=MESH)
+
+    @pl.loop(1, device_count)
+    def _(step):
+        flat = lax.rem(me + step, device_count)
+        peer = {"node": flat // (2 * z_count), "local": lax.rem(flat, 2 * z_count)}
+        pl.semaphore_signal(barrier, inc=1, device_id=peer, device_id_type=MESH)
 
     target = []
     for p in range(z_count):
@@ -200,11 +198,42 @@
         copy.start()
         extra_copies.append(copy)
 
+    def partner(p, i):
+        other_core = core if i // 2 == 0 else 1 - core
+        other_local = target[p] * 2 + (y if i % 2 == 0 else 1 - y)
+        return other_core, other_local, other_core * 2 * z_count + other_local
+
+    def a_copy(p, i):
+        other_core, other_local, flat = partner(p, i)
+        return pltpu.make_async_remote_copy(
+            send_ref.at[flat], arrived.at[me], a_send.at[flat], a_recv.at[me],
+            device_id={"node": other_core, "local": other_local}, device_id_type=MESH,
+        )
+
+    def a_arrival(p, i):
+        _, _, flat = partner(p, i)
+        return pltpu.make_async_remote_copy(
+            send_ref.at[flat], arrived.at[flat], a_send.at[flat], a_recv.at[flat],
+            device_id=core_peer, device_id_type=MESH,
+        )
+
+    own_rows = pltpu.make_async_copy(send_ref.at[me], arrived.at[me], a_recv.at[me])
+    own_rows.start()
+    exchanged = [(p, i) for p in range(z_count) for i in range(4) if (p, i) != (z_count - 1, 0)]
+    pl.semaphore_wait(barrier, device_count - 1)
+    for p, i in exchanged:
+        a_copy(p, i).start()
+
     def compute(p):
         zt = target[p]
         for i in range(4):
+            if (p, i) in exchanged:
+                a_arrival(p, i).wait_recv()
+            else:
+                own_rows.wait()
+        for i in range(4):
             origin = (i // 2) * 2 * z_count + zt * 2 + i % 2
-            rows = jnp.dot(unpack_ref[origin], arrived_ref[origin], preferred_element_type=f32)
+            rows = jnp.dot(unpack_ref[origin], arrived[origin], preferred_element_type=f32)
             lhs[pl.ds(i * tok_rows, tok_rows), :] = rows.astype(bf16)
         low[...] = lax.dot_general(
             lhs[...], second_ref[...], nt, preferred_element_type=f32
@@ -256,8 +285,6 @@
                 y_copy(p).start()
 
     compute(0)
-    neighbours = 2 + jnp.where(z > 0, 1, 0) + jnp.where(z < z_count - 1, 1, 0)
-    pl.semaphore_wait(barrier, neighbours)
     c_copy(0).start()
     for p in range(1, z_count):
         compute(p)
@@ -341,6 +368,8 @@
     def _():
         finish(True, True)
 
+    for p, i in exchanged:
+        a_copy(p, i).wait_send()
     for p in range(z_count):
         c_copy(p).wait_send()
         y_copy(p).wait_send()
@@ -348,7 +377,7 @@
         z_copy(p, 0, local).wait_send()
 
 
-def return_sums(arrived, unpack, frozen, first, second, extra, tok_rows):
+def return_sums(send_g, unpack, frozen, first, second, extra, tok_rows):
     bf16 = jnp.bfloat16
     z_count, more, width = extra.shape[1], extra.shape[3], extra.shape[4]
     rows = tok_rows + more
@@ -361,15 +390,17 @@
             jax.ShapeDtypeStruct((tok_rows, width), bf16),
             jax.ShapeDtypeStruct((more, width), jnp.float32),
         ),
-        in_specs=[vmem] * 5 + [pl.BlockSpec(memory_space=pl.ANY)],
+        in_specs=[pl.BlockSpec(memory_space=pl.ANY)] + [vmem] * 4 + [pl.BlockSpec(memory_space=pl.ANY)],
         out_specs=(vmem, vmem),
         scratch_shapes=[
+            pltpu.VMEM(send_g.shape, bf16),
             pltpu.VMEM((z_count, 2, 2, rows, width), bf16),
             pltpu.VMEM((z_count, 2, rows, width), bf16),
             pltpu.VMEM((z_count, rows, width), bf16),
             pltpu.VMEM((z_count + 1, rows, width), bf16),
             pltpu.VMEM((4 * tok_rows, frozen.shape[1]), bf16),
             pltpu.VMEM((4 * tok_rows, second.shape[0]), bf16),
+            dma((4 * z_count,)), dma((4 * z_count,)),
             dma((z_count,)), dma((z_count,)), dma((z_count,)), dma((z_count,)),
             dma((z_count,)), dma((z_count,)), dma((z_count + 1,)),
         ],
@@ -379,7 +410,7 @@
         cost_estimate=pl.CostEstimate(
             flops=2 * routes * width * frozen.shape[1], bytes_accessed=20 * 2**20, transcendentals=0
         ),
-    )(arrived, unpack, frozen, first, second, extra)
+    )(send_g, unpack, frozen, first, second, extra)
 
 
 def gather_kernel(z_count, own_ref, all_ref, own_sem, recv, up_send, down_send, y_send, c_send):
@@ -543,12 +574,8 @@
     slots = jnp.arange(device_count * slot_most, dtype=jnp.int32)
     pack = (target.reshape(1, -1) == slots[:, None]).astype(bf16)
     send_g = jnp.dot(pack, scaled, preferred_element_type=f32).astype(bf16)
+    send_g = send_g.reshape(device_count, slot_most, hidden)
     own = jnp.concatenate([first_t, second, table], axis=1)
-    own, send_g = lax.optimization_barrier((own, send_g))
-    arrived = lax.all_to_all(
-        send_g.reshape(device_count, slot_most, hidden), axes, split_axis=0, concat_axis=0, tiled=True
-    )
-
     shared = gather_shards(own, device_count)
     all_first = shared[:, :width]
     all_second = shared[:, width : width + hidden]
@@ -579,7 +606,7 @@
         mine[:, :, None] & (place[:, :, None] == jnp.arange(slot_most, dtype=jnp.int32))
     ).astype(bf16)
     input_grad, factor_sums = return_sums(
-        arrived, unpack, frozen_up[0], factor_a[0] * adapter_scale_factor, second, extra, tok_rows
+        send_g, unpack, frozen_up[0], factor_a[0] * adapter_scale_factor, second, extra, tok_rows
     )
     factor_sums = factor_sums * (weight_gradient_total * adapter_scale_factor)
     grad_a = factor_sums[:rank].T[None]

time: 264 us -> 239 us (0.905)
  Pallas kernels: 225 us -> 210 us
  starting transfers between devices: 6.31 us -> 0 us
  matrix products: 14.4 us -> 10.9 us
    pallas_call x1, Pallas kernels: 83.2 us -> 31.3 us  [gather_shards(): pl.pallas_call(functools.partial(gather_kernel, z_count), out_shape=jax.S...]
    pallas_call x1, Pallas kernels: 142 us -> 179 us  [return_sums(): pl.pallas_call(functools.partial(return_kernel, z_count), out_shape=(jax....]
    all_to_all x1 -> x0, starting transfers between devices: 6.31 us -> none  [dense_body(): lax.all_to_all(send_g.reshape(device_count, slot_most, hidden), axes, spl...]
  transfers between devices with their start and end apart: 1 -> 0, of which waited for: 0 -> 0; matrix products, arithmetic and copies ran while one was open for 6% -> 0% of each run, Pallas kernels for 32% -> 0%
where the time goes in v4:
time: 239 us
  Pallas kernels  210 us (88%)
  other arithmetic  12.2 us (5%)
  matrix products  10.9 us (5%)
  local copies, waits for them, and re-layouts  4.64 us (2%)
    pallas_call x1, Pallas kernels, return_sums(): pl.pallas_call(functools.partial(return_kernel, z_count), out_shape=(jax....  179 us
    pallas_call x1, Pallas kernels, gather_shards(): pl.pallas_call(functools.partial(gather_kernel, z_count), out_shape=jax.S...  31.3 us

profile of v4, /device:TPU:8, one launch (start us, length us, event | category | flops | bytes accessed | tf_op | source)
XLA Modules:
  0.0 239.0 jit_solution(14588495379057154793)
XLA Ops:
  0.6 0.0 copy-start
  0.7 0.8 broadcast_multiply_fusion.1
  1.4 0.7 convert_bitcast_fusion
  2.2 0.1 eq.94
  2.2 0.1 copy.40
  2.3 0.2 reduce_window_sum.22
  2.5 0.1 copy.41
  2.6 0.1 copy.42
  2.7 0.1 eq.83
  2.8 0.1 copy.46
  2.9 0.1 eq.92
  3.0 0.8 copy.43
  3.8 1.0 fusion.31.own_ref
  4.8 1.4 copy.44
  6.2 1.0 bitcast_multiply_fusion.first_ref
  7.2 2.0 multiply_convert_fusion
  9.2 4.2 %fusion.1 = bf16[1280,1024]{1,0:T(8,128)(2,1)} fusion(s32[1024]{0:T(1024)S(1)} %eq.83, bf16[128,8,1024]{2,1,0:T(8,128)(2,1)S(1)} %multiply_convert_fusion), kind=kOutput, calls=%fused_computation.5 | convolution fusion | flops 2686976000 | bytes 4722688 | tf_op jit(solution)/shard_map/dot_general | solution.py:576
  13.4 31.3 %shard_map.103 = bf16[2,4,2,32,4736]{4,3,2,1,0:T(8,128)(2,1)S(1)} custom-call(bf16[32,4736]{1,0:T(8,128)(2,1)S(1)} %fusion.31.own_ref), custom_call_target="tpu_custom_call" | custom-call | bytes 104857600 | tf_op jit(solution)/shard_map/pallas_call | solution.py:526
  44.7 1.7 bitcast_reduce_fusion
  46.4 0.0 copy-done
  46.4 1.1 fusion.20
  47.5 2.8 %bitcast_convert_fusion = bf16[512,1024]{1,0:T(8,128)(2,1)S(1)} fusion(bf16[128,8,1024]{2,1,0:T(8,128)(2,1)S(1)} %multiply_convert_fusion, s32[128,8]{0,1:T(8,128)S(1)} %get-tuple-element.20, s32[512]{0:T(512)S(1)} %eq.94, bf16[128,512]{0,1:T(8,128)(2,1)S(1)} %fusion.20), kind=kOutput, calls=%fused_computation.12 | convolution fusion | flops 1075314688 | bytes 3282944 | tf_op jit(solution)/shard_map/dot_general | solution.py:594
  50.4 0.1 slice_bitcast_fusion.1
  50.5 0.3 reduce_window_sum.23
  50.8 1.4 fusion.27.unpack_ref
  52.2 0.2 fusion.12
  52.4 1.1 convolution_convert_fusion
  53.5 2.7 %pad_maximum_fusion.extra_ref = bf16[2,4,2,48,3584]{4,3,2,1,0:T(8,128)(2,1)} fusion(bf16[2,4,2,16,3584]{4,3,2,1,0:T(8,128)(2,1)S(1)} %bitcast.49, bf16[2,4,2,32,3584]{4,3,2,1,0:T(8,128)(2,1)S(1)} %bitcast.48), kind=kLoop, calls=%fused_computation.1 | loop fusion | flops 11010048 | bytes 11010048 | tf_op jit(solution)/shard_map/concatenate | solution.py:599
  56.3 179.1 %shard_map.104 = (bf16[128,3584]{1,0:T(8,128)(2,1)}, f32[48,3584]{1,0:T(8,128)}) custom-call(bf16[16,80,1024]{2,1,0:T(8,128)(2,1)} %bitcast.57, bf16[16,128,80]{2,1,0:T(8,128)(2,1)} %fusion.27.unpack_ref, bf16[3584,1024]{1,0:T(8,128)(2,1)} %bitcast.56, bf16[3584,32]{1,0:T(8,128)(2,1)} %bitcast_multiply_fusion.first_ref, bf16[32,1024]{1,0:T(8,128)(2,1)} %bitcast.54, ...), custom_call_target="tpu_custom_call" | custom-call | flops 15032385536 | bytes 20971520 | tf_op jit(solution)/shard_map/pallas_call | solution.py:387
  235.4 0.0 copy-start.1
  235.4 1.2 broadcast_multiply_fusion
  236.6 0.8 slice_bitcast_fusion.2
  237.4 0.7 maximum_bitcast_fusion
  238.1 0.0 copy-done.1
  238.1 0.9 copy.58
  (12 shorter events, 0.2 us)
Async XLA Ops:
  0.6 45.7 %copy-start = (bf16[128,3584]{1,0:T(8,128)(2,1)S(1)}, bf16[128,3584]{1,0:T(8,128)(2,1)}, u32[]{:S(2)}) copy-start(bf16[128,3584]{1,0:T(8,128)(2,1)} %param.10) | copy-start | bytes 2752516
  235.4 2.7 %copy-start.1 = (bf16[128,3584]{1,0:T(8,128)(2,1)S(1)}, bf16[128,3584]{1,0:T(8,128)(2,1)}, u32[]{:S(2)}) copy-start(bf16[128,3584]{1,0:T(8,128)(2,1)} %get-tuple-element.28) | copy-start | bytes 2752516

commit v5 on v4

--- a/solution.py
+++ b/solution.py
@@ -221,8 +221,18 @@
     own_rows.start()
     exchanged = [(p, i) for p in range(z_count) for i in range(4) if (p, i) != (z_count - 1, 0)]
     pl.semaphore_wait(barrier, device_count - 1)
-    for p, i in exchanged:
-        a_copy(p, i).start()
+
+    def send_rows(p):
+        for i in range(4):
+            if (p, i) in exchanged:
+                a_copy(p, i).start()
+
+    send_rows(0)
+    for i in range(4):
+        if (0, i) in exchanged:
+            a_copy(0, i).wait_send()
+    if z_count > 1:
+        send_rows(1)
 
     def compute(p):
         zt = target[p]
@@ -231,6 +241,9 @@
                 a_arrival(p, i).wait_recv()
             else:
                 own_rows.wait()
+        if p == 0:
+            for later in range(2, z_count):
+                send_rows(later)
         for i in range(4):
             origin = (i // 2) * 2 * z_count + zt * 2 + i % 2
             rows = jnp.dot(unpack_ref[origin], arrived[origin], preferred_element_type=f32)
@@ -369,7 +382,8 @@
         finish(True, True)
 
     for p, i in exchanged:
-        a_copy(p, i).wait_send()
+        if p > 0:
+            a_copy(p, i).wait_send()
     for p in range(z_count):
         c_copy(p).wait_send()
         y_copy(p).wait_send()

time: 239 us -> 241 us (level)
  no operation moved by 1% of the time
where the time goes in v5:
time: 241 us; the launch traced here: 240 us
  Pallas kernels  212 us (88%)
  other arithmetic  12.2 us (5%)
  matrix products  10.9 us (5%)
  local copies, waits for them, and re-layouts  4.64 us (2%)
    pallas_call x1, Pallas kernels, return_sums(): pl.pallas_call(functools.partial(return_kernel, z_count), out_shape=(jax....  180 us
    pallas_call x1, Pallas kernels, gather_shards(): pl.pallas_call(functools.partial(gather_kernel, z_count), out_shape=jax.S...  31.3 us

profile of v5, /device:TPU:8, one launch (start us, length us, event | category | flops | bytes accessed | tf_op | source)
XLA Modules:
  0.0 240.3 jit_solution(3996136494062397598)
XLA Ops:
  0.6 0.0 copy-start
  0.7 0.8 broadcast_multiply_fusion.1
  1.4 0.7 convert_bitcast_fusion
  2.2 0.1 eq.94
  2.2 0.1 copy.40
  2.3 0.2 reduce_window_sum.22
  2.5 0.1 copy.41
  2.6 0.1 copy.42
  2.7 0.1 eq.83
  2.8 0.1 copy.46
  2.9 0.1 eq.92
  3.0 0.8 copy.43
  3.8 1.0 fusion.31.own_ref
  4.8 1.4 copy.44
  6.2 1.0 bitcast_multiply_fusion.first_ref
  7.2 2.0 multiply_convert_fusion
  9.2 4.2 %fusion.1 = bf16[1280,1024]{1,0:T(8,128)(2,1)} fusion(s32[1024]{0:T(1024)S(1)} %eq.83, bf16[128,8,1024]{2,1,0:T(8,128)(2,1)S(1)} %multiply_convert_fusion), kind=kOutput, calls=%fused_computation.5 | convolution fusion | flops 2686976000 | bytes 4722688 | tf_op jit(solution)/shard_map/dot_general | solution.py:590
  13.4 31.3 %shard_map.103 = bf16[2,4,2,32,4736]{4,3,2,1,0:T(8,128)(2,1)S(1)} custom-call(bf16[32,4736]{1,0:T(8,128)(2,1)S(1)} %fusion.31.own_ref), custom_call_target="tpu_custom_call" | custom-call | bytes 104857600 | tf_op jit(solution)/shard_map/pallas_call | solution.py:540
  44.7 1.7 bitcast_reduce_fusion
  46.4 0.0 copy-done
  46.4 1.1 fusion.20
  47.5 2.8 %bitcast_convert_fusion = bf16[512,1024]{1,0:T(8,128)(2,1)S(1)} fusion(bf16[128,8,1024]{2,1,0:T(8,128)(2,1)S(1)} %multiply_convert_fusion, s32[128,8]{0,1:T(8,128)S(1)} %get-tuple-element.20, s32[512]{0:T(512)S(1)} %eq.94, bf16[128,512]{0,1:T(8,128)(2,1)S(1)} %fusion.20), kind=kOutput, calls=%fused_computation.12 | convolution fusion | flops 1075314688 | bytes 3282944 | tf_op jit(solution)/shard_map/dot_general | solution.py:608
  50.4 0.1 slice_bitcast_fusion.1
  50.5 0.3 reduce_window_sum.23
  50.8 1.4 fusion.27.unpack_ref
  52.2 0.2 fusion.12
  52.4 1.1 convolution_convert_fusion
  53.5 2.7 %pad_maximum_fusion.extra_ref = bf16[2,4,2,48,3584]{4,3,2,1,0:T(8,128)(2,1)} fusion(bf16[2,4,2,16,3584]{4,3,2,1,0:T(8,128)(2,1)S(1)} %bitcast.49, bf16[2,4,2,32,3584]{4,3,2,1,0:T(8,128)(2,1)S(1)} %bitcast.48), kind=kLoop, calls=%fused_computation.1 | loop fusion | flops 11010048 | bytes 11010048 | tf_op jit(solution)/shard_map/concatenate | solution.py:613
  56.3 180.4 %shard_map.104 = (bf16[128,3584]{1,0:T(8,128)(2,1)}, f32[48,3584]{1,0:T(8,128)}) custom-call(bf16[16,80,1024]{2,1,0:T(8,128)(2,1)} %bitcast.57, bf16[16,128,80]{2,1,0:T(8,128)(2,1)} %fusion.27.unpack_ref, bf16[3584,1024]{1,0:T(8,128)(2,1)} %bitcast.56, bf16[3584,32]{1,0:T(8,128)(2,1)} %bitcast_multiply_fusion.first_ref, bf16[32,1024]{1,0:T(8,128)(2,1)} %bitcast.54, ...), custom_call_target="tpu_custom_call" | custom-call | flops 15032385536 | bytes 20971520 | tf_op jit(solution)/shard_map/pallas_call | solution.py:401
  236.7 0.0 copy-start.1
  236.7 1.2 broadcast_multiply_fusion
  237.9 0.8 slice_bitcast_fusion.2
  238.7 0.7 maximum_bitcast_fusion
  239.4 0.0 copy-done.1
  239.4 0.9 copy.58
  (12 shorter events, 0.2 us)
Async XLA Ops:
  0.6 45.7 %copy-start = (bf16[128,3584]{1,0:T(8,128)(2,1)S(1)}, bf16[128,3584]{1,0:T(8,128)(2,1)}, u32[]{:S(2)}) copy-start(bf16[128,3584]{1,0:T(8,128)(2,1)} %param.10) | copy-start | bytes 2752516
  236.7 2.7 %copy-start.1 = (bf16[128,3584]{1,0:T(8,128)(2,1)S(1)}, bf16[128,3584]{1,0:T(8,128)(2,1)}, u32[]{:S(2)}) copy-start(bf16[128,3584]{1,0:T(8,128)(2,1)} %get-tuple-element.28) | copy-start | bytes 2752516

commit v6 on v4

--- a/solution.py
+++ b/solution.py
@@ -413,7 +413,9 @@
     )(send_g, unpack, frozen, first, second, extra)
 
 
-def gather_kernel(z_count, own_ref, all_ref, own_sem, recv, up_send, down_send, y_send, c_send):
+def gather_kernel(
+    z_count, own_ref, pack_ref, scaled_ref, all_ref, rows_ref, own_sem, recv, up_send, down_send, y_send, c_send
+):
     core = lax.axis_index("node")
     local = lax.axis_index("local")
     z, y = local // 2, lax.rem(local, 2)
@@ -489,6 +491,12 @@
 
             spread(zs)
 
+    @pl.loop(0, rows_ref.shape[0])
+    def _(i):
+        rows_ref[i] = jnp.dot(
+            pack_ref[i], scaled_ref[...], preferred_element_type=jnp.float32
+        ).astype(rows_ref.dtype)
+
     def from_y(zs):
         arrival(core, zs, 1 - y)
         copy(zs, 1 - y, c_send.at[zs, 1 - y], core_peer).start()
@@ -519,25 +527,28 @@
             copy(zs, y, down_send.at[zs], core_peer).wait_send()
 
 
-def gather_shards(own, device_count):
+def gather_shards(own, pack, scaled, device_count):
     z_count = device_count // 4
     dma = pltpu.SemaphoreType.DMA
     vmem = pl.BlockSpec(memory_space=pltpu.VMEM)
-    gathered = pl.pallas_call(
+    gathered, rows = pl.pallas_call(
         functools.partial(gather_kernel, z_count),
-        out_shape=jax.ShapeDtypeStruct((2, z_count, 2) + own.shape, own.dtype),
-        in_specs=[vmem],
-        out_specs=vmem,
+        out_shape=(
+            jax.ShapeDtypeStruct((2, z_count, 2) + own.shape, own.dtype),
+            jax.ShapeDtypeStruct(pack.shape[:2] + scaled.shape[1:], scaled.dtype),
+        ),
+        in_specs=[vmem] * 3,
+        out_specs=(vmem, vmem),
         scratch_shapes=[
             dma, dma((2, z_count, 2)), dma((z_count,)), dma((z_count,)),
             dma((z_count,)), dma((z_count, 2)),
         ],
         compiler_params=pltpu.CompilerParams(
-            collective_id=1, has_side_effects=True, vmem_limit_bytes=24 * 2**20
+            collective_id=1, has_side_effects=True, vmem_limit_bytes=40 * 2**20
         ),
         cost_estimate=pl.CostEstimate(flops=0, bytes_accessed=100 * 2**20, transcendentals=0),
-    )(own)
-    return gathered.reshape((device_count * own.shape[0],) + own.shape[1:])
+    )(own, pack, scaled)
+    return gathered.reshape((device_count * own.shape[0],) + own.shape[1:]), rows
 
 
 def scale_routes(grads, route_weights):
@@ -573,10 +584,9 @@
     scaled = scale_routes(grads, route_weights)
     slots = jnp.arange(device_count * slot_most, dtype=jnp.int32)
     pack = (target.reshape(1, -1) == slots[:, None]).astype(bf16)
-    send_g = jnp.dot(pack, scaled, preferred_element_type=f32).astype(bf16)
-    send_g = send_g.reshape(device_count, slot_most, hidden)
+    pack = pack.reshape(device_count, slot_most, -1)
     own = jnp.concatenate([first_t, second, table], axis=1)
-    shared = gather_shards(own, device_count)
+    shared, send_g = gather_shards(own, pack, scaled, device_count)
     all_first = shared[:, :width]
     all_second = shared[:, width : width + hidden]
     tables = shared[:, width + hidden :].reshape(device_count, rank, tok_rows)[:, :topk]

time: 239 us -> 252 us (1.054)
  local copies, waits for them, and re-layouts: 4.64 us -> 9.94 us
  other arithmetic: 12.2 us -> 16.5 us
  Pallas kernels: 210 us -> 213 us
    unnamed x7 -> x19, local copies, waits for them, and re-layouts: 3.09 us -> 8.42 us
    dot_general x1 -> x0, matrix products: 4.17 us -> none  [dense_body(): send_g = jnp.dot(pack, scaled, preferred_element_type=f32).astype(bf16)]
    pallas_call x1, Pallas kernels: 179 us -> 182 us  [return_sums(): pl.pallas_call(functools.partial(return_kernel, z_count), out_shape=(jax....]
where the time goes in v6:
time: 252 us; the launch traced here: 251 us
  Pallas kernels  213 us (85%)
  other arithmetic  16.5 us (7%)
  matrix products  10.8 us (4%)
  local copies, waits for them, and re-layouts  9.94 us (4%)
    pallas_call x1, Pallas kernels, return_sums(): pl.pallas_call(functools.partial(return_kernel, z_count), out_shape=(jax....  182 us
    pallas_call x1, Pallas kernels, gather_shards(): pl.pallas_call(functools.partial(gather_kernel, z_count), out_shape=(jax....  31.4 us
    unnamed x19, local copies, waits for them, and re-layouts  8.42 us

profile of v6, /device:TPU:8, one launch (start us, length us, event | category | flops | bytes accessed | tf_op | source)
XLA Modules:
  0.0 251.4 jit_solution(103201595882004047)
XLA Ops:
  0.6 0.0 copy-start
  0.6 0.8 broadcast_multiply_fusion.1
  1.4 0.7 convert_bitcast_fusion
  2.1 1.7 fusion.23.own_ref
  3.9 0.1 copy.42
  4.0 0.2 reduce_window_sum.22
  4.1 0.1 copy.43
  4.2 0.1 copy.44
  4.3 0.1 eq.90
  4.4 0.5 compare_convert_fusion.pack_ref
  4.9 1.4 copy.45
  6.4 0.0 copy-start.1
  6.4 2.1 fusion.32.scaled_ref
  8.4 0.0 copy-done.1
  8.5 31.4 %shard_map.103 = (bf16[2,4,2,32,4736]{4,3,2,1,0:T(8,128)(2,1)S(1)}, bf16[16,80,1024]{2,1,0:T(8,128)(2,1)S(1)}) custom-call(bf16[32,4736]{1,0:T(8,128)(2,1)S(1)} %copy-done.1, bf16[16,80,1024]{2,1,0:T(8,128)(2,1)S(1)} %compare_convert_fusion.pack_ref, bf16[1024,1024]{1,0:T(8,128)(2,1)S(1)} %fusion.32.scaled_ref), custom_call_target="tpu_custom_call" | custom-call | bytes 104857600 | tf_op jit(solution)/shard_map/pallas_call | solution.py:534
  39.8 0.0 copy-start.3
  39.8 1.5 copy-done.3
  41.3 0.0 copy-start.2
  41.3 0.0 copy-start.4
  41.3 0.0 copy-start.7
  41.3 2.4 copy-done.2
  43.8 0.3 reduce_window_sum.23
  44.1 1.4 fusion.19.unpack_ref
  45.5 2.2 copy.40
  47.7 2.2 bitcast_multiply_fusion.first_ref
  49.8 0.0 copy-done.4
  49.8 0.0 copy-done.7
  49.8 1.8 multiply_convert_fusion
  51.6 0.1 eq.104
  51.7 0.0 copy-done
  51.7 0.0 copy-start.5
  51.7 3.3 %fusion.12 = bf16[128,512]{0,1:T(8,128)(2,1)S(1)} fusion(bf16[128,3584]{1,0:T(8,128)(2,1)S(1)} %copy-done, bf16[512,4736]{1,0:T(8,128)(2,1)} %bitcast.42), kind=kOutput, calls=%fused_computation.16 | convolution fusion | flops 469827584 | bytes 4718592 | tf_op jit(solution)/shard_map/dot_general | solution.py:597
  55.0 0.0 copy-done.5
  55.0 2.8 %bitcast_convert_fusion = bf16[512,1024]{1,0:T(8,128)(2,1)S(1)} fusion(bf16[128,8,1024]{2,1,0:T(8,128)(2,1)S(1)} %copy-done.5, s32[128,8]{0,1:T(8,128)S(1)} %get-tuple-element.24, s32[512]{0:T(512)S(1)} %eq.104, bf16[128,512]{0,1:T(8,128)(2,1)S(1)} %fusion.12), kind=kOutput, calls=%fused_computation.9 | convolution fusion | flops 1075314688 | bytes 3282944 | tf_op jit(solution)/shard_map/dot_general | solution.py:604
  57.8 0.1 slice_bitcast_fusion.1
  57.9 0.2 fusion.6
  58.1 0.1 copy.46
  58.2 0.1 eq.102
  58.3 3.5 %bitcast_reduce_fusion = bf16[128,512]{1,0:T(8,128)(2,1)S(1)} fusion(bf16[512,4736]{1,0:T(8,128)(2,1)} %bitcast.43, s32[512]{0:T(512)S(1)} %eq.104, s32[1024]{0:T(1024)S(1)} %eq.102, bf16[128,8,1024]{2,1,0:T(8,128)(2,1)} %multiply_convert_fusion), kind=kOutput, calls=%fused_computation.10 | convolution fusion | flops 1075249152 | bytes 3282944 | tf_op jit(solution)/shard_map/dot_general | solution.py:595
  61.8 1.1 convolution_convert_fusion
  63.0 2.8 %pad_maximum_fusion.extra_ref = bf16[2,4,2,48,3584]{4,3,2,1,0:T(8,128)(2,1)} fusion(bf16[2,4,2,16,3584]{4,3,2,1,0:T(8,128)(2,1)S(1)} %bitcast.45, bf16[2,4,2,32,3584]{4,3,2,1,0:T(8,128)(2,1)S(1)} %bitcast.44), kind=kLoop, calls=%fused_computation.1 | loop fusion | flops 11010048 | bytes 11010048 | tf_op jit(solution)/shard_map/concatenate | solution.py:609
  65.7 182.1 %shard_map.104 = (bf16[128,3584]{1,0:T(8,128)(2,1)}, f32[48,3584]{1,0:T(8,128)}) custom-call(bf16[16,80,1024]{2,1,0:T(8,128)(2,1)} %copy-done.3, bf16[16,128,80]{2,1,0:T(8,128)(2,1)} %fusion.19.unpack_ref, bf16[3584,1024]{1,0:T(8,128)(2,1)} %bitcast.52, bf16[3584,32]{1,0:T(8,128)(2,1)} %bitcast_multiply_fusion.first_ref, bf16[32,1024]{1,0:T(8,128)(2,1)} %bitcast.50, ...), custom_call_target="tpu_custom_call" | custom-call | flops 15032385536 | bytes 20971520 | tf_op jit(solution)/shard_map/pallas_call | solution.py:387
  247.8 0.0 copy-start.6
  247.8 1.2 broadcast_multiply_fusion
  249.0 0.8 slice_bitcast_fusion.2
  249.9 0.7 maximum_bitcast_fusion
  250.5 0.0 copy-done.6
  250.5 0.9 copy.58
  (13 shorter events, 0.2 us)
Async XLA Ops:
  0.6 51.1 %copy-start = (bf16[128,3584]{1,0:T(8,128)(2,1)S(1)}, bf16[128,3584]{1,0:T(8,128)(2,1)}, u32[]{:S(2)}) copy-start(bf16[128,3584]{1,0:T(8,128)(2,1)} %param.10) | copy-start | bytes 2752516
  6.4 2.1 copy-start.1
  39.8 1.5 copy-start.3
  41.3 2.4 copy-start.2
  41.3 8.5 %copy-start.4 = (bf16[128,8,1024]{2,1,0:T(8,128)(2,1)S(1)}, bf16[128,8,1024]{2,1,0:T(8,128)(2,1)}, u32[]{:S(2)}) copy-start(bf16[128,8,1024]{2,1,0:T(8,128)(2,1)} %param.11) | copy-start | bytes 6291460
  41.3 8.5 %copy-start.7 = (f32[128,8]{1,0:T(8,128)S(1)}, f32[128,8]{1,0:T(8,128)}, u32[]{:S(2)}) copy-start(f32[128,8]{1,0:T(8,128)} %copy.45) | copy-start | bytes 12292
  51.7 3.3 %copy-start.5 = (bf16[128,8,1024]{2,1,0:T(8,128)(2,1)S(1)}, bf16[128,8,1024]{2,1,0:T(8,128)(2,1)}, u32[]{:S(2)}) copy-start(bf16[128,8,1024]{2,1,0:T(8,128)(2,1)} %multiply_convert_fusion) | copy-start | bytes 6291460
  247.8 2.7 %copy-start.6 = (bf16[128,3584]{1,0:T(8,128)(2,1)S(1)}, bf16[128,3584]{1,0:T(8,128)(2,1)}, u32[]{:S(2)}) copy-start(bf16[128,3584]{1,0:T(8,128)(2,1)} %get-tuple-element.32) | copy-start | bytes 2752516
